TPU v7x, 32 devices: a whole 2x2x4 slice. The times are simulated.
32 devices in a mesh: groups: 2 (over x), row: 16 (over z, y, core).
Axes of the slice: x: 2, y: 2, z: 4, core: 2. Of those that a mesh axis runs over, the one named last changes fastest.
Arguments:
- pair: bfloat16 [256, 128, 128], P('groups', 'row'), parts along dimension 0, may hold values from -6 to 6
- residue_mask: int32 [256], P('groups'), parts along dimension 0, may hold values 0 or 1
- ln_in_gain: float32 [128], replicated, may hold values from 0.1 to 1.9
- ln_in_bias: float32 [128], replicated, may hold values from -1.5 to 1.5
- w_edges: bfloat16 [128, 256], replicated, may hold values from -0.5 to 0.5
- w_edge_gates: bfloat16 [128, 256], replicated, may hold values from -0.5 to 0.5
- ln_out_gain: float32 [128], replicated, may hold values from 0.1 to 1.9
- ln_out_bias: float32 [128], replicated, may hold values from -1.5 to 1.5
- w_gate: bfloat16 [128, 128], replicated, may hold values from -0.5 to 0.5
- w_out: bfloat16 [128, 128], replicated, may hold values from -0.5 to 0.5
Outputs:
- update: bfloat16 [256, 128, 128], P('groups', 'row'), parts along dimension 0
There are 2 independent parts, one for each index of `groups`. A program takes and returns all parts, laid end to end along the dimension named above; an argument that names none is the same for every part. Nothing has to cross between parts.
All inputs are finite; a program needn't handle non-finite values.
Results may differ from a plain program's by a relative error of at most 0.0072.
Values may be sent and summed in bfloat16 or wider, within the bound.
No kernel may reach another device: no remote copies, remote signals or barrier semaphores. Data moves between devices by JAX's collectives and lax.ppermute only.
A program may use at most 128 MiB of HBM per device.

v0:
```python
import jax
import jax.numpy as jnp
from jax import lax
from jax.sharding import PartitionSpec as P


def layer_norm(values, gain, bias):
    mean = jnp.mean(values, axis=-1, keepdims=True)
    centered = values - mean
    spread = jnp.mean(centered * centered, axis=-1, keepdims=True)
    return centered * lax.rsqrt(spread + 1e-05) * gain + bias


def local(
    pair,
    residue_mask,
    ln_in_gain,
    ln_in_bias,
    w_edges,
    w_edge_gates,
    ln_out_gain,
    ln_out_bias,
    w_gate,
    w_out,
):
    columns = pair.shape[1]
    first = lax.axis_index("row") * columns
    normed = layer_norm(pair.astype(jnp.float32), ln_in_gain, ln_in_bias).astype(jnp.bfloat16)
    proj = jnp.einsum("ijc,cd->ijd", normed, w_edges, preferred_element_type=jnp.float32)
    gates = jnp.einsum("ijc,cd->ijd", normed, w_edge_gates, preferred_element_type=jnp.float32)
    valid = residue_mask.astype(jnp.float32)
    col_valid = lax.dynamic_slice_in_dim(valid, first, columns, 0)
    pair_valid = valid[:, None, None] * col_valid[None, :, None]
    edges = (jax.nn.sigmoid(gates) * proj * pair_valid).astype(jnp.bfloat16)
    hidden = edges.shape[2] // 2
    left = edges[:, :, :hidden]
    right = edges[:, :, hidden:]
    right_mine = lax.all_to_all(right, "row", split_axis=0, concat_axis=1, tiled=True)
    outer = jnp.einsum(
        "ikc,jkc->ijc",
        lax.all_gather(left, "row", axis=1, tiled=True),
        right_mine,
        preferred_element_type=jnp.float32,
    )
    outer_normed = layer_norm(outer, ln_out_gain, ln_out_bias).astype(jnp.bfloat16)
    gate = jax.nn.sigmoid(
        jnp.einsum("ijc,cd->ijd", normed, w_gate, preferred_element_type=jnp.float32)
    )
    projected = jnp.einsum("ijc,cd->ijd", outer_normed, w_out, preferred_element_type=jnp.float32)
    return (gate * projected).astype(jnp.bfloat16)


def solution(mesh):
    return jax.shard_map(
        local,
        mesh=mesh,
        in_specs=(P("groups", "row", None), P("groups"), P(), P(), P(), P(), P(), P(), P(), P()),
        out_specs=P("groups", "row", None),
        check_vma=False,
    )
```

profile of v0, /device:TPU:0, one launch (start us, length us, event | category | flops | bytes accessed | tf_op | source)
XLA Modules:
  0.0 89.2 jit_solution(5491494564090828956)
XLA Ops:
  6.5 0.7 convert_element_type.20
  7.2 0.1 dynamic_slice.3
  7.3 0.1 broadcast_multiply_fusion
  7.4 1.2 %convert_reduce_fusion = f32[128,8]{1,0:T(8,128)S(1)} fusion(bf16[128,8,128]{2,1,0:T(8,128)(2,1)} %param.10), kind=kLoop, calls=%fused_computation.15 | loop fusion | flops 261120 | bytes 266240 | tf_op jit(solution)/shard_map/reduce_sum | solution.py:8
  8.6 0.1 copy.64
  8.7 1.3 %fusion.12 = f32[128,8]{1,0:T(8,128)S(1)} fusion(bf16[128,8,128]{2,1,0:T(8,128)(2,1)} %param.10, f32[128,8]{1,0:T(8,128)S(1)} %copy.64), kind=kLoop, calls=%fused_computation.18 | loop fusion | flops 523264 | bytes 270336 | tf_op jit(solution)/shard_map/reduce_sum | solution.py:10
  10.1 0.1 copy.66
  10.2 1.3 %fusion.15 = bf16[128,8,128]{2,1,0:T(8,128)(2,1)S(1)} fusion(bf16[128,8,128]{2,1,0:T(8,128)(2,1)} %param.10, f32[128]{0:T(128)} %param.13, f32[128]{0:T(128)} %param.12, f32[128,8]{1,0:T(8,128)S(1)} %copy.66, f32[128,8]{1,0:T(8,128)S(1)} %copy.64), kind=kLoop, calls=%fused_computation.21 | loop fusion | flops 786432 | bytes 533504 | tf_op jit(solution)/shard_map/convert_element_type | solution.py:28
  11.6 0.3 fusion.17
  11.8 1.3 %fusion.5 = bf16[128,8,256]{2,0,1:T(8,128)(2,1)S(1)} fusion(f32[128,8,256]{2,0,1:T(8,128)S(1)} %fusion.17, f32[128,8]{0,1:T(8,128)S(1)} %broadcast_multiply_fusion, bf16[128,8,128]{2,1,0:T(8,128)(2,1)S(1)} %fusion.15, bf16[128,256]{1,0:T(8,128)(2,1)} %param.15), kind=kOutput, calls=%fused_computation.6 | convolution fusion | flops 68681728 | bytes 1904640 | tf_op jit(solution)/shard_map/ijc,cd->ijd/dot_general | solution.py:30
  13.1 0.8 fusion.25
  14.0 0.0 all-gather.2.cloned.1.call-update
  14.0 0.9 copy.70
  14.9 7.4 %all-to-all-start = ((bf16[128,8,128]{2,1,0:T(8,128)(2,1)}), bf16[128,8,128]{2,1,0:T(8,128)(2,1)S(1)}, u32[]{:S(2)}, u32[]{:S(2)}) async-start(bf16[128,8,128]{2,1,0:T(8,128)(2,1)} %copy.70), calls=%async_computation | async-start | bytes 524288 | tf_op jit(solution)/shard_map/all_to_all | solution.py:38
  22.3 0.3 fusion.8
  22.6 12.0 %all-to-all-done = bf16[128,8,128]{2,1,0:T(8,128)(2,1)S(1)} async-done(((bf16[128,8,128]{2,1,0:T(8,128)(2,1)}), bf16[128,8,128]{2,1,0:T(8,128)(2,1)S(1)}, u32[]{:S(2)}, u32[]{:S(2)}) %all-to-all-start) | async-done | bytes 262176 | tf_op jit(solution)/shard_map/all_to_all | solution.py:38
  34.6 0.2 copy.72
  34.8 35.7 %all-gather.2.cloned.1.call-done = bf16[128,128,128]{2,0,1:T(8,128)(2,1)} async-done(((bf16[128,8,128]{2,0,1:T(8,128)(2,1)}), bf16[128,128,128]{2,0,1:T(8,128)(2,1)}) %all-gather.2.cloned.1.call-update) | async-done | bytes 4194320 | tf_op jit(solution)/shard_map/all_gather | solution.py:41
  70.5 6.7 %copy.73 = bf16[128,128,128]{0,1,2:T(8,128)(2,1)} copy(bf16[128,128,128]{2,0,1:T(8,128)(2,1)} %all-gather.2.cloned.1.call-done) | data formatting | bytes 8388608 | tf_op jit(solution)/shard_map/all_gather | solution.py:41
  77.3 3.4 %fusion.26 = (f32[128,8]{0,1:T(8,128)S(1)}, f32[128,8,128]{0,1,2:T(8,128)S(1)}) fusion(bf16[8,128,128]{1,0,2:T(8,128)(2,1)S(1)} %copy.72, bf16[128,128,128]{0,1,2:T(8,128)(2,1)} %copy.73), kind=kOutput, calls=%fused_computation.40 | convolution fusion | flops 33684480 | bytes 4984832 | tf_op jit(solution)/shard_map/ikc,jkc->ijc/dot_general | solution.py:39
  80.7 0.1 multiply_reduce_fusion
  80.9 0.3 add_convert_fusion
  81.2 0.3 fusion.9
  81.5 0.9 copy.75
  (18 shorter events, 0.2 us)
Async XLA Ops:
  6.5 5.0 %copy-start = (bf16[128,256]{1,0:T(8,128)(2,1)S(1)}, bf16[128,256]{1,0:T(8,128)(2,1)}, u32[]{:S(2)}) copy-start(bf16[128,256]{1,0:T(8,128)(2,1)} %param.14) | copy-start | bytes 196612
  6.5 64.0 %all-gather.2.cloned.1.call-start = ((), (), s32[]{:S(2)}) async-start(), calls=%async_computation.1 | async-start | bytes 4456448 | tf_op jit(solution)/shard_map/all_gather | solution.py:41
  11.6 10.7 %copy-start.4 = (bf16[128,128]{1,0:T(8,128)(2,1)S(1)}, bf16[128,128]{1,0:T(8,128)(2,1)}, u32[]{:S(2)}) copy-start(bf16[128,128]{1,0:T(8,128)(2,1)} %param.18) | copy-start | bytes 98308
  14.9 19.7 %all-to-all-start = ((bf16[128,8,128]{2,1,0:T(8,128)(2,1)}), bf16[128,8,128]{2,1,0:T(8,128)(2,1)S(1)}, u32[]{:S(2)}, u32[]{:S(2)}) async-start(bf16[128,8,128]{2,1,0:T(8,128)(2,1)} %copy.70), calls=%async_computation | async-start | bytes 524288 | tf_op jit(solution)/shard_map/all_to_all | solution.py:38
  77.3 3.6 %copy-start.2 = (f32[128]{0:T(128)S(1)}, f32[128]{0:T(128)}, u32[]{:S(2)}) copy-start(f32[128]{0:T(128)} %param.17) | copy-start | bytes 1540
  77.3 3.6 %copy-start.3 = (f32[128]{0:T(128)S(1)}, f32[128]{0:T(128)}, u32[]{:S(2)}) copy-start(f32[128]{0:T(128)} %param.16) | copy-start | bytes 1540
  77.3 3.9 %copy-start.1 = (bf16[128,128]{1,0:T(8,128)(2,1)S(1)}, bf16[128,128]{1,0:T(8,128)(2,1)}, u32[]{:S(2)}) copy-start(bf16[128,128]{1,0:T(8,128)(2,1)} %param.19) | copy-start | bytes 98308
Sparse Core Ops, SparseCore 0:
  14.1 56.3 all-gather.1
where the time goes:
time: 89.7 us; the launch traced here: 89.2 us
  waiting for transfers between devices  47.7 us (53%)
  between operations  13.5 us (15%)
  local copies, waits for them, and re-layouts  9.97 us (11%)
  starting transfers between devices  7.4 us (8%)
  matrix products  5.51 us (6%)
  other arithmetic  5.06 us (6%)
    all_gather x1, waiting for transfers between devices, local(): lax.all_gather(left, 'row', axis=1, tiled=True)  35.7 us
    all_to_all x1, waiting for transfers between devices, local(): lax.all_to_all(right, 'row', split_axis=0, concat_axis=1, tiled=True)  12 us
    all_to_all x1, starting transfers between devices, local(): lax.all_to_all(right, 'row', split_axis=0, concat_axis=1, tiled=True)  7.4 us
    all_gather x1, local copies, waits for them, and re-layouts, local(): lax.all_gather(left, 'row', axis=1, tiled=True)  6.74 us
    dot_general x1, matrix products, local(): jnp.einsum('ikc,jkc->ijc', lax.all_gather(left, 'row', axis=1, tiled=True...  3.41 us
  transfers between devices with their start and end apart: 2, of which 2 were waited for; matrix products, arithmetic and copies ran while one was open for 2% of the time, Pallas kernels for 0%

commit v1 on v0

v1 whole, which is shorter than its diff:
```python
import functools

import jax
import jax.numpy as jnp
from jax import lax
from jax.experimental import pallas as pl
from jax.experimental.pallas import tpu as pltpu
from jax.sharding import PartitionSpec as P

SQUARE = 8
PEERS = (2, 4, 6)
F32, BF16 = jnp.float32, jnp.bfloat16
VMEM = pl.BlockSpec(memory_space=pltpu.VMEM)
SMEM = pl.BlockSpec(memory_space=pltpu.SMEM)


def dot(a, b):
    return lax.dot_general(a, b, (((1,), (0,)), ((), ())), preferred_element_type=F32)


def row_means(values):
    lanes = values.shape[1]
    high = values.astype(BF16)
    low = (values - high.astype(F32)).astype(BF16)
    ones = jnp.full((2 * lanes, lanes), 1.0 / lanes, BF16)
    return dot(jnp.concatenate([high, low], axis=1), ones)


def sigmoid(x):
    return 0.5 + 0.5 * jnp.tanh(0.5 * x)


def layer_norm(values, mean, gain, bias):
    centered = values - mean
    spread = row_means(centered * centered)
    return (centered * lax.rsqrt(spread + 1e-05) * gain + bias).astype(BF16)


def input_norm(x, gain, bias):
    lanes = x.shape[1]
    mean = dot(x, jnp.full((lanes, lanes), 1.0 / lanes, BF16))
    return layer_norm(x.astype(F32), mean, gain, bias)


def gated(normed, w):
    half = w.shape[1] // 2
    both = dot(normed, w)
    return both[:, :half] * sigmoid(both[:, half:])


def k_valid(mask_ref, first, columns, lanes):
    at = lax.broadcasted_iota(jnp.int32, (columns, lanes), 0)
    out = jnp.zeros((columns, lanes), F32)
    for n in range(columns):
        out = jnp.where(at == n, mask_ref[first + n].astype(F32), out)
    return out


def right_edges(normed_ref, first, rows, w, valid):
    right = gated(normed_ref[pl.ds(first, rows), :], w)
    columns, lanes = valid.shape
    return (right.reshape(rows // columns, columns, lanes) * valid).reshape(rows, lanes)


def contract(lefts, right_ref, j_first, js, put, block, columns):
    at_once = 4
    chip_js = right_ref.shape[0] // len(lefts) // columns

    def step(g, carry):
        sums = [None] * at_once
        for s, (ref, first) in enumerate(lefts):
            for k in range(columns):
                left = ref[pl.ds(first + k, block, stride=columns), :]
                for n in range(at_once):
                    at = (s * chip_js + j_first + g * at_once + n) * columns + k
                    term = left * right_ref[pl.ds(at, 1), :]
                    sums[n] = term if sums[n] is None else sums[n] + term
        for n in range(at_once):
            put(g * at_once + n, sums[n])
        return carry

    lax.fori_loop(0, js // at_once, step, 0)


def split_weights(we_ref, wg_ref):
    half = we_ref.shape[1] // 2
    left = jnp.concatenate([we_ref[:, :half], wg_ref[:, :half]], axis=1)
    right = jnp.concatenate([we_ref[:, half:], wg_ref[:, half:]], axis=1)
    return left, right


def own_kernel(squares, block, columns, me_ref, mask_ref, pair_ref, gain_ref, bias_ref, we_ref, wg_ref, gate_ref, left_ref, right_ref, gates_ref, normed_ref):
    me = me_ref[0]
    lanes = pair_ref.shape[1]
    rows, js = block * columns, 2 * columns * columns
    w_left, w_right = split_weights(we_ref, wg_ref)
    valid = k_valid(mask_ref, me * columns, columns, lanes)
    for t in range(squares):
        x = pair_ref[pl.ds(pl.multiple_of(((me // SQUARE) ^ t) * rows, rows), rows), :]
        normed = input_norm(x, gain_ref[...], bias_ref[...])
        normed_ref[...] = normed
        left_ref[t * rows : (t + 1) * rows, :] = gated(normed, w_left)
        gates_ref[t * rows : (t + 1) * rows, :] = sigmoid(dot(normed, gate_ref[...]))
        first = pl.multiple_of(((me // 2) % (SQUARE // 2)) * js, js)
        right_ref[t * js : (t + 1) * js, :] = right_edges(normed_ref, first, js, w_right, valid)


def chunk_kernel(t, earlier, block, columns, *refs):
    me_ref, mask_ref, *refs = refs
    slabs, refs = refs[: len(PEERS)], refs[len(PEERS) :]
    own_left_ref, own_right_ref, gain_ref, bias_ref, we_ref, wg_ref, *refs = refs
    old_rights, refs = refs[: len(earlier)], refs[len(earlier) :]
    left_ref, right_ref, *refs = refs
    targets = list(earlier) + ([t] if t else [])
    outs, (normed_ref,) = refs[: 2 * len(targets)], refs[2 * len(targets) :]
    me = me_ref[0]
    lanes = left_ref.shape[1]
    rows, js = block * columns, 2 * columns * columns
    w_left, w_right = split_weights(we_ref, wg_ref)
    first = pl.multiple_of(((me // 2) % (SQUARE // 2)) * js, js)
    right_ref[:js, :] = own_right_ref[t * js : (t + 1) * js, :]
    for n, slab in enumerate(slabs):
        normed = input_norm(slab[...], gain_ref[...], bias_ref[...])
        normed_ref[n] = normed
        left_ref[n * rows : (n + 1) * rows, :] = gated(normed, w_left)
        valid = k_valid(mask_ref, (me ^ PEERS[n]) * columns, columns, lanes)
        right_ref[(n + 1) * js : (n + 2) * js, :] = right_edges(normed_ref.at[n], first, js, w_right, valid)
    lefts = [(own_left_ref, t * rows)] + [(left_ref, n * rows) for n in range(len(slabs))]
    rights = list(old_rights) + ([right_ref] if t else [])
    for n, right in enumerate(rights):
        both_cores(lefts, right, me % 2, outs[2 * n], outs[2 * n + 1], block, columns)


def both_cores(lefts, right, core, send_ref, keep_ref, block, columns):
    def put_send(j, value):
        send_ref[pl.ds(pl.multiple_of(j * block, block), block), :] = value.astype(BF16)

    def put_keep(j, value):
        keep_ref[pl.ds(pl.multiple_of(j * block, block), block), :] = value

    contract(lefts, right, (1 - core) * columns, columns, put_send, block, columns)
    contract(lefts, right, core * columns, columns, put_keep, block, columns)


def late_kernel(pairs, block, columns, *refs):
    n_left = 1 + max(p[1] for p in pairs)
    n_right = 1 + max(p[2] for p in pairs)
    me_ref, own_left_ref, *refs = refs
    lefts, refs = refs[:n_left], refs[n_left:]
    rights, outs = refs[:n_right], refs[n_right:]
    rows = block * columns
    for n, (t, a, b) in enumerate(pairs):
        slabs = [(own_left_ref, t * rows)] + [(lefts[a], m * rows) for m in range(len(PEERS))]
        both_cores(slabs, rights[b], me_ref[0] % 2, outs[2 * n], outs[2 * n + 1], block, columns)


def last_kernel(squares, block, columns, *refs):
    me_ref, mask_ref, mask_row_ref, *refs = refs
    each = squares + 1
    sums, refs = refs[: squares * each], refs[squares * each :]
    gates_ref, gain_ref, bias_ref, w_ref, out_ref, turned_ref = refs
    me = me_ref[0]
    rows = block * columns
    lanes = out_ref.shape[1]
    residues = mask_row_ref.shape[1]
    for t in range(squares):
        first = ((me // SQUARE) ^ t) * block
        at = lax.broadcasted_iota(jnp.int32, (block, residues), 0) + first
        chosen = jnp.where(lax.broadcasted_iota(jnp.int32, (block, residues), 1) == at, mask_row_ref[...], 0)
        valid = dot(chosen.astype(F32).astype(BF16), jnp.ones((residues, lanes), BF16))
        for j in range(columns):
            here = pl.ds(j * block, block)
            outer = sums[t * each][here, :]
            for other in sums[t * each + 1 : (t + 1) * each]:
                outer = outer + other[here, :].astype(F32)
            outer = outer * (valid * mask_ref[me * columns + j].astype(F32))
            normed = layer_norm(outer, row_means(outer), gain_ref[...], bias_ref[...])
            turned_ref[pl.ds(j, block, stride=columns), :] = dot(normed, w_ref[...])
        update = turned_ref[...] * gates_ref[t * rows : (t + 1) * rows, :]
        out_ref[pl.ds(pl.multiple_of(first * columns, rows), rows), :] = update.astype(BF16)


def call(kernel, operands, specs, outs, scratch=(), cost=1e6):
    return pl.pallas_call(
        kernel,
        out_shape=[jax.ShapeDtypeStruct(shape, dtype) for shape, dtype in outs],
        in_specs=specs,
        out_specs=[VMEM] * len(outs),
        scratch_shapes=list(scratch),
        cost_estimate=pl.CostEstimate(flops=int(cost), bytes_accessed=1 << 20, transcendentals=0),
        compiler_params=pltpu.CompilerParams(vmem_limit_bytes=32 << 20),
    )(*operands)


def local(size, pair, residue_mask, ln_in_gain, ln_in_bias, w_edges, w_edge_gates, ln_out_gain, ln_out_bias, w_gate, w_out):
    residues, columns, lanes = pair.shape
    squares = size // SQUARE
    block = residues // squares
    rows, js = block * columns, 2 * columns * columns
    index = lax.axis_index("row")
    me = index.astype(jnp.int32).reshape(1)
    square = index // SQUARE

    def swap(value, bits):
        return lax.ppermute(value, "row", [(i, i ^ bits) for i in range(size)])

    in_gain, in_bias = ln_in_gain.reshape(1, lanes), ln_in_bias.reshape(1, lanes)
    order = list(range(1, squares)) + [0]
    slabs = {}
    for t in order:
        own = lax.dynamic_slice_in_dim(pair, (square ^ t) * block, block, 0).reshape(rows, lanes)
        slabs[t] = [swap(own, bits) for bits in PEERS]

    with jax.named_scope("own_edges"):
        own_left, own_right, gates = call(
            functools.partial(own_kernel, squares, block, columns),
            (me, residue_mask, pair.reshape(residues * columns, lanes), in_gain, in_bias, w_edges, w_edge_gates, w_gate),
            [SMEM, SMEM] + [VMEM] * 6,
            [((squares * rows, lanes), F32), ((squares * js, lanes), F32), ((squares * rows, lanes), F32)],
            [pltpu.VMEM((rows, lanes), BF16)],
        )

    lefts, rights, parts, arrived = {}, {}, {}, {}

    def share(t, s, send, keep):
        other = swap(send, 1)
        if s == 0:
            parts[t, 0] = [keep, other]
        else:
            arrived[t ^ s, s] = swap((keep + other.astype(F32)).astype(BF16), SQUARE * s)

    piece = [((rows, lanes), BF16), ((rows, lanes), F32)]
    done = set()
    for t in order:
        earlier = tuple(s for s in rights if s)
        targets = earlier + ((t,) if t else ())
        with jax.named_scope("chunk"):
            lefts[t], rights[t], *made = call(
                functools.partial(chunk_kernel, t, earlier, block, columns),
                (me, residue_mask, *slabs[t], own_left, own_right, in_gain, in_bias, w_edges, w_edge_gates, *(rights[s] for s in earlier)),
                [SMEM, SMEM] + [VMEM] * (len(PEERS) + 6 + len(earlier)),
                [((len(PEERS) * rows, lanes), F32), ((SQUARE // 2 * js, lanes), F32)] + piece * len(targets),
                [pltpu.VMEM((len(PEERS), rows, lanes), BF16)],
            )
        for n, s in enumerate(targets):
            share(t, s, made[2 * n], made[2 * n + 1])
            done.add((t, s))
    left_over = [(t, s) for s in order for t in order if (t, s) not in done]
    with jax.named_scope("own_outer"):
        made = call(
            functools.partial(late_kernel, [(t, order.index(t), order.index(s)) for t, s in left_over], block, columns),
            (me, own_left, *(lefts[t] for t in order), *(rights[t] for t in order)),
            [SMEM] + [VMEM] * (1 + 2 * squares),
            piece * len(left_over),
        )
    for n, (t, s) in enumerate(left_over):
        share(t, s, made[2 * n], made[2 * n + 1])

    with jax.named_scope("update"):
        sums = []
        for t in range(squares):
            sums += parts[t, 0] + [arrived[t, s] for s in range(1, squares)]
        (update,) = call(
            functools.partial(last_kernel, squares, block, columns),
            (me, residue_mask, residue_mask.reshape(1, residues), *sums, gates, ln_out_gain.reshape(1, lanes), ln_out_bias.reshape(1, lanes), w_out),
            [SMEM, SMEM] + [VMEM] * (5 + len(sums)),
            [((residues * columns, lanes), BF16)],
            [pltpu.VMEM((rows, lanes), F32)],
        )
    return update.reshape(residues, columns, lanes)


def solution(mesh):
    return jax.shard_map(
        functools.partial(local, mesh.shape["row"]),
        mesh=mesh,
        in_specs=(P("groups", "row", None), P("groups"), P(), P(), P(), P(), P(), P(), P(), P()),
        out_specs=P("groups", "row", None),
        check_vma=False,
    )
```

time: 89.7 us -> 45.7 us (0.51)
  waiting for transfers between devices: 47.7 us -> 12.8 us
  Pallas kernels: 0 us -> 15.4 us
  between operations: 13.5 us -> 0.11 us
  local copies, waits for them, and re-layouts: 9.97 us -> 2.37 us
  starting transfers between devices: 7.4 us -> 14.7 us
  matrix products: 5.51 us -> 0 us
  other arithmetic: 5.06 us -> 0.07 us
    all_gather x1 -> x0, waiting for transfers between devices: 35.7 us -> none  [local(): lax.all_gather(left, 'row', axis=1, tiled=True)]
    pallas_call x0 -> x5, Pallas kernels: none -> 15.4 us  [call(): pl.pallas_call(kernel, out_shape=[jax.ShapeDtypeStruct(shape, dtype) for...]
    ppermute x0 -> x12, starting transfers between devices: none -> 14.7 us  [swap(): return lax.ppermute(value, 'row', [(i, i ^ bits) for i in range(size)])]
    ppermute x0 -> x12, waiting for transfers between devices: none -> 12.8 us  [swap(): return lax.ppermute(value, 'row', [(i, i ^ bits) for i in range(size)])]
    all_to_all x1 -> x0, waiting for transfers between devices: 12 us -> none  [local(): lax.all_to_all(right, 'row', split_axis=0, concat_axis=1, tiled=True)]
    all_to_all x1 -> x0, starting transfers between devices: 7.4 us -> none  [local(): lax.all_to_all(right, 'row', split_axis=0, concat_axis=1, tiled=True)]
    all_gather x1 -> x0, local copies, waits for them, and re-layouts: 6.74 us -> none  [local(): lax.all_gather(left, 'row', axis=1, tiled=True)]
    dot_general x5 -> x0, matrix products: 5.51 us -> none  [the longest x1 3.41 us: local(): jnp.einsum('ikc,jkc->ijc', lax.all_gather(left, 'row', axis=1, tiled=True...]
  transfers between devices with their start and end apart: 2 -> 12, of which waited for: 2 -> 4; matrix products, arithmetic and copies ran while one was open for 2% -> 0% of each run, Pallas kernels for 0% -> 25%
where the time goes in v1:
time: 45.7 us; the launch traced here: 45.5 us
  Pallas kernels  15.4 us (34%)
  starting transfers between devices  14.7 us (32%)
  waiting for transfers between devices  12.8 us (28%)
  local copies, waits for them, and re-layouts  2.37 us (5%)
    pallas_call x5, Pallas kernels, call(): pl.pallas_call(kernel, out_shape=[jax.ShapeDtypeStruct(shape, dtype) for...  15.4 us
    ppermute x12, starting transfers between devices, swap(): return lax.ppermute(value, 'row', [(i, i ^ bits) for i in range(size)])  14.7 us
    ppermute x12, waiting for transfers between devices, swap(): return lax.ppermute(value, 'row', [(i, i ^ bits) for i in range(size)])  12.8 us
    unnamed x20, local copies, waits for them, and re-layouts  1.33 us
    reshape x1, local copies, waits for them, and re-layouts, local(): lax.dynamic_slice_in_dim(pair, (square ^ t) * block, block, 0)  1.04 us
  transfers between devices with their start and end apart: 12, of which 4 were waited for; matrix products, arithmetic and copies ran while one was open for 0% of the time, Pallas kernels for 25%

profile of v1, /device:TPU:0, one launch (start us, length us, event | category | flops | bytes accessed | tf_op | source)
XLA Modules:
  0.0 45.5 jit_solution(11348756314622991848)
XLA Ops:
  0.0 1.0 %dynamic-slice_bitcast_fusion = (bf16[512,128]{1,0:T(8,128)(2,1)S(1)}, bf16[512,128]{1,0:T(8,128)(2,1)S(1)}) fusion(bf16[128,8,128]{2,1,0:T(8,128)(2,1)} %param.10, s32[]{:T(128)S(6)} %select_n.13, s32[]{:T(128)S(6)} %select_n.12), kind=kLoop, calls=%fused_computation.2 | loop fusion | bytes 524296 | tf_op jit(solution)/shard_map/reshape | solution.py:211
  1.0 4.1 %collective-permute-start.2 = (bf16[512,128]{1,0:T(8,128)(2,1)S(1)}, bf16[512,128]{1,0:T(8,128)(2,1)S(1)}, u32[]{:S(2)}, u32[]{:S(2)}) collective-permute-start(bf16[512,128]{1,0:T(8,128)(2,1)S(1)} %get-tuple-element.36), channel_id=1, source_target_pairs={{0,6},{1,7},{2,4},{3,5},{4,2},{5,3},{6,0},{7,1},{8,14},{9,15},{10,... | collective-permute-start | bytes 393224 | tf_op jit(solution)/shard_map/ppermute | solution.py:205
  5.1 0.4 collective-permute-start.1
  5.6 0.2 collective-permute-start
  5.7 2.8 %collective-permute-start.5 = (bf16[512,128]{1,0:T(8,128)(2,1)S(1)}, bf16[512,128]{1,0:T(8,128)(2,1)S(1)}, u32[]{:S(2)}, u32[]{:S(2)}) collective-permute-start(bf16[512,128]{1,0:T(8,128)(2,1)S(1)} %get-tuple-element.35), channel_id=1, source_target_pairs={{0,6},{1,7},{2,4},{3,5},{4,2},{5,3},{6,0},{7,1},{8,14},{9,15},{10,... | collective-permute-start | bytes 393224 | tf_op jit(solution)/shard_map/ppermute | solution.py:205
  8.6 0.4 collective-permute-start.4
  9.0 0.4 collective-permute-done.2.refs_4_
  9.4 1.9 %collective-permute-start.3 = (bf16[512,128]{1,0:T(8,128)(2,1)S(1)}, bf16[512,128]{1,0:T(8,128)(2,1)S(1)}, u32[]{:S(2)}, u32[]{:S(2)}) collective-permute-start(bf16[512,128]{1,0:T(8,128)(2,1)S(1)} %get-tuple-element.35), channel_id=1, source_target_pairs={{0,2},{1,3},{2,0},{3,1},{4,6},{5,7},{6,4},{7,5},{8,10},{9,11},{10,... | collective-permute-start | bytes 393224 | tf_op jit(solution)/shard_map/ppermute | solution.py:205
  11.4 0.6 %copy-done.5 = s32[128]{0:T(128)S(1)} copy-done((s32[128]{0:T(128)S(1)}, s32[128]{0:T(128)}, u32[]{:S(2)}) %copy-start.5) | copy-done | bytes 536
  12.1 1.5 %own_edges.1 = (f32[1024,128]{1,0:T(8,128)S(1)}, f32[256,128]{1,0:T(8,128)S(1)}, f32[1024,128]{1,0:T(8,128)S(1)}) custom-call(s32[1]{0:T(128)} %bitcast.me_ref.refs_0_, s32[128]{0:T(128)S(1)} %copy-done.5, bf16[1024,128]{1,0:T(8,128)(2,1)S(1)} %bitcast.12, f32[1,128]{1,0:T(1,128)S(1)} %bitcast.14, f32[1,128]{1,0:T(1,128)S(1)} %bitcast.17, ...), custom_call_target="tpu_custom_call" | custom-call | flops 1000000 | bytes 1048576 | tf_op jit(solution)/shard_map/own_edges/pallas_call | solution.py:184
  13.6 1.3 %collective-permute-done.refs_2_ = bf16[512,128]{1,0:T(8,128)(2,1)S(1)} collective-permute-done((bf16[512,128]{1,0:T(8,128)(2,1)S(1)}, bf16[512,128]{1,0:T(8,128)(2,1)S(1)}, u32[]{:S(2)}, u32[]{:S(2)}) %collective-permute-start) | collective-permute-done | bytes 131104 | tf_op jit(solution)/shard_map/ppermute | solution.py:205
  14.8 3.4 %chunk.2 = (f32[1536,128]{1,0:T(8,128)S(1)}, f32[512,128]{1,0:T(8,128)S(1)}, bf16[512,128]{1,0:T(8,128)(2,1)S(1)}, f32[512,128]{1,0:T(8,128)S(1)}) custom-call(s32[1]{0:T(128)} %bitcast.me_ref.refs_0_, s32[128]{0:T(128)S(1)} %copy-done.5, bf16[512,128]{1,0:T(8,128)(2,1)S(1)} %collective-permute-done.refs_2_, ...), custom_call_target="tpu_custom_call" | custom-call | flops 1000000 | bytes 1048576 | tf_op jit(solution)/shard_map/chunk/pallas_call | solution.py:184
  18.2 0.1 collective-permute-start.7
  18.3 3.4 %chunk.3 = (f32[1536,128]{1,0:T(8,128)S(1)}, f32[512,128]{1,0:T(8,128)S(1)}, bf16[512,128]{1,0:T(8,128)(2,1)S(1)}, f32[512,128]{1,0:T(8,128)S(1)}) custom-call(s32[1]{0:T(128)} %bitcast.me_ref.refs_0_, s32[128]{0:T(128)S(1)} %copy-done.5, bf16[512,128]{1,0:T(8,128)(2,1)S(1)} %collective-permute-done.3.refs_2_, ...), custom_call_target="tpu_custom_call" | custom-call | flops 1000000 | bytes 1048576 | tf_op jit(solution)/shard_map/chunk/pallas_call | solution.py:184
  21.8 3.0 %own_outer.1 = (bf16[512,128]{1,0:T(8,128)(2,1)S(1)}, f32[512,128]{1,0:T(8,128)S(1)}, bf16[512,128]{1,0:T(8,128)(2,1)S(1)}, f32[512,128]{1,0:T(8,128)S(1)}) custom-call(s32[1]{0:T(128)} %bitcast.me_ref.refs_0_, f32[1024,128]{1,0:T(8,128)S(1)} %get-tuple-element.20.refs_5_.refs_1_, f32[1536,128]{1,0:T(8,128)S(1)} %get-tuple-element.22.refs_2_, ...), custom_call_target="tpu_custom_call" | custom-call | flops 1000000 | bytes 1048576 | tf_op jit(solution)/shard_map/own_outer/pallas_call | solution.py:184
  24.8 0.5 %collective-permute-start.6 = (bf16[512,128]{1,0:T(8,128)(2,1)S(1)}, bf16[512,128]{1,0:T(8,128)(2,1)S(1)}, u32[]{:S(2)}, u32[]{:S(2)}) collective-permute-start(bf16[512,128]{1,0:T(8,128)(2,1)S(1)} %get-tuple-element.27), channel_id=1, source_target_pairs={{0,1},{1,0},{2,3},{3,2},{4,5},{5,4},{6,7},{7,6},{8,9},{9,8},{10,11... | collective-permute-start | bytes 393224 | tf_op jit(solution)/shard_map/ppermute | solution.py:205
  25.3 0.1 collective-permute-start.9
  25.4 0.4 collective-permute-start.10
  25.9 2.7 %collective-permute-start.8 = (bf16[512,128]{1,0:T(8,128)(2,1)S(1)}, bf16[512,128]{1,0:T(8,128)(2,1)S(1)}, u32[]{:S(2)}, u32[]{:S(2)}) collective-permute-start(bf16[512,128]{1,0:T(8,128)(2,1)S(1)} %add_convert_fusion.1), channel_id=1, source_target_pairs={{0,8},{1,9},{2,10},{3,11},{4,12},{5,13},{6,14},{7,15},{8,0},{9,1},... | collective-permute-start | bytes 393224 | tf_op jit(solution)/shard_map/ppermute | solution.py:205
  28.6 1.0 %collective-permute-start.11 = (bf16[512,128]{1,0:T(8,128)(2,1)S(1)}, bf16[512,128]{1,0:T(8,128)(2,1)S(1)}, u32[]{:S(2)}, u32[]{:S(2)}) collective-permute-start(bf16[512,128]{1,0:T(8,128)(2,1)S(1)} %add_convert_fusion), channel_id=1, source_target_pairs={{0,8},{1,9},{2,10},{3,11},{4,12},{5,13},{6,14},{7,15},{8,0},{9,1},... | collective-permute-start | bytes 393224 | tf_op jit(solution)/shard_map/ppermute | solution.py:205
  29.6 9.2 %collective-permute-done.8.refs_5_ = bf16[512,128]{1,0:T(8,128)(2,1)S(1)} collective-permute-done((bf16[512,128]{1,0:T(8,128)(2,1)S(1)}, bf16[512,128]{1,0:T(8,128)(2,1)S(1)}, u32[]{:S(2)}, u32[]{:S(2)}) %collective-permute-start.8) | collective-permute-done | bytes 131104 | tf_op jit(solution)/shard_map/ppermute | solution.py:205
  38.8 1.9 %collective-permute-done.11.refs_8_ = bf16[512,128]{1,0:T(8,128)(2,1)S(1)} collective-permute-done((bf16[512,128]{1,0:T(8,128)(2,1)S(1)}, bf16[512,128]{1,0:T(8,128)(2,1)S(1)}, u32[]{:S(2)}, u32[]{:S(2)}) %collective-permute-start.11) | collective-permute-done | bytes 131104 | tf_op jit(solution)/shard_map/ppermute | solution.py:205
  40.7 0.6 %copy-done.8 = f32[128]{0:T(128)S(1)} copy-done((f32[128]{0:T(128)S(1)}, f32[128]{0:T(128)}, u32[]{:S(2)}) %copy-start.8) | copy-done | bytes 536
  41.4 4.1 %update.1 = bf16[1024,128]{1,0:T(8,128)(2,1)} custom-call(s32[1]{0:T(128)} %bitcast.me_ref.refs_0_, s32[128]{0:T(128)S(1)} %copy-done.5, s32[1,128]{1,0:T(1,128)S(1)} %bitcast.13, f32[512,128]{1,0:T(8,128)S(1)} %get-tuple-element.26.refs_3_, bf16[512,128]{1,0:T(8,128)(2,1)S(1)} %collective-permute-done.6.refs_4_, ...), custom_call_target="tpu_custom_call" | custom-call | flops 1000000 | bytes 1048576 | tf_op jit(solution)/shard_map/update/pallas_call | solution.py:184
  (28 shorter events, 0.2 us)
Async XLA Ops:
  0.0 11.4 %copy-start = (bf16[128,8,128]{2,1,0:T(8,128)(2,1)S(1)}, bf16[128,8,128]{2,1,0:T(8,128)(2,1)}, u32[]{:S(2)}) copy-start(bf16[128,8,128]{2,1,0:T(8,128)(2,1)} %param.10) | copy-start | bytes 786436
  0.0 11.4 %copy-start.1 = (bf16[128,256]{1,0:T(8,128)(2,1)S(1)}, bf16[128,256]{1,0:T(8,128)(2,1)}, u32[]{:S(2)}) copy-start(bf16[128,256]{1,0:T(8,128)(2,1)} %refs_9_.3) | copy-start | bytes 196612
  0.0 11.4 %copy-start.2 = (bf16[128,256]{1,0:T(8,128)(2,1)S(1)}, bf16[128,256]{1,0:T(8,128)(2,1)}, u32[]{:S(2)}) copy-start(bf16[128,256]{1,0:T(8,128)(2,1)} %refs_10_.3) | copy-start | bytes 196612
  0.0 11.4 %copy-start.4 = (bf16[128,128]{1,0:T(8,128)(2,1)S(1)}, bf16[128,128]{1,0:T(8,128)(2,1)}, u32[]{:S(2)}) copy-start(bf16[128,128]{1,0:T(8,128)(2,1)} %gate_ref.1) | copy-start | bytes 98308
  1.0 8.4 %collective-permute-start.2 = (bf16[512,128]{1,0:T(8,128)(2,1)S(1)}, bf16[512,128]{1,0:T(8,128)(2,1)S(1)}, u32[]{:S(2)}, u32[]{:S(2)}) collective-permute-start(bf16[512,128]{1,0:T(8,128)(2,1)S(1)} %get-tuple-element.36), channel_id=1, source_target_pairs={{0,6},{1,7},{2,4},{3,5},{4,2},{5,3},{6,0},{7,1},{8,14},{9,15},{10,... | collective-permute-start | bytes 393224 | tf_op jit(solution)/shard_map/ppermute | solution.py:205
  5.1 8.4 %collective-permute-start.1 = (bf16[512,128]{1,0:T(8,128)(2,1)S(1)}, bf16[512,128]{1,0:T(8,128)(2,1)S(1)}, u32[]{:S(2)}, u32[]{:S(2)}) collective-permute-start(bf16[512,128]{1,0:T(8,128)(2,1)S(1)} %get-tuple-element.36), channel_id=1, source_target_pairs={{0,4},{1,5},{2,6},{3,7},{4,0},{5,1},{6,2},{7,3},{8,12},{9,13},{10,... | collective-permute-start | bytes 393224 | tf_op jit(solution)/shard_map/ppermute | solution.py:205
  5.6 9.3 %collective-permute-start = (bf16[512,128]{1,0:T(8,128)(2,1)S(1)}, bf16[512,128]{1,0:T(8,128)(2,1)S(1)}, u32[]{:S(2)}, u32[]{:S(2)}) collective-permute-start(bf16[512,128]{1,0:T(8,128)(2,1)S(1)} %get-tuple-element.36), channel_id=1, source_target_pairs={{0,2},{1,3},{2,0},{3,1},{4,6},{5,7},{6,4},{7,5},{8,10},{9,11},{10,... | collective-permute-start | bytes 393224 | tf_op jit(solution)/shard_map/ppermute | solution.py:205
  5.7 12.6 %collective-permute-start.5 = (bf16[512,128]{1,0:T(8,128)(2,1)S(1)}, bf16[512,128]{1,0:T(8,128)(2,1)S(1)}, u32[]{:S(2)}, u32[]{:S(2)}) collective-permute-start(bf16[512,128]{1,0:T(8,128)(2,1)S(1)} %get-tuple-element.35), channel_id=1, source_target_pairs={{0,6},{1,7},{2,4},{3,5},{4,2},{5,3},{6,0},{7,1},{8,14},{9,15},{10,... | collective-permute-start | bytes 393224 | tf_op jit(solution)/shard_map/ppermute | solution.py:205
  8.6 9.7 %collective-permute-start.4 = (bf16[512,128]{1,0:T(8,128)(2,1)S(1)}, bf16[512,128]{1,0:T(8,128)(2,1)S(1)}, u32[]{:S(2)}, u32[]{:S(2)}) collective-permute-start(bf16[512,128]{1,0:T(8,128)(2,1)S(1)} %get-tuple-element.35), channel_id=1, source_target_pairs={{0,4},{1,5},{2,6},{3,7},{4,0},{5,1},{6,2},{7,3},{8,12},{9,13},{10,... | collective-permute-start | bytes 393224 | tf_op jit(solution)/shard_map/ppermute | solution.py:205
  9.4 8.9 %collective-permute-start.3 = (bf16[512,128]{1,0:T(8,128)(2,1)S(1)}, bf16[512,128]{1,0:T(8,128)(2,1)S(1)}, u32[]{:S(2)}, u32[]{:S(2)}) collective-permute-start(bf16[512,128]{1,0:T(8,128)(2,1)S(1)} %get-tuple-element.35), channel_id=1, source_target_pairs={{0,2},{1,3},{2,0},{3,1},{4,6},{5,7},{6,4},{7,5},{8,10},{9,11},{10,... | collective-permute-start | bytes 393224 | tf_op jit(solution)/shard_map/ppermute | solution.py:205
  11.4 0.7 %copy-start.5 = (s32[128]{0:T(128)S(1)}, s32[128]{0:T(128)}, u32[]{:S(2)}) copy-start(s32[128]{0:T(128)} %refs_1_.5) | copy-start | bytes 1540
  11.4 0.7 %copy-start.6 = (f32[128]{0:T(128)S(1)}, f32[128]{0:T(128)}, u32[]{:S(2)}) copy-start(f32[128]{0:T(128)} %param.12) | copy-start | bytes 1540
  11.4 0.7 %copy-start.7 = (f32[128]{0:T(128)S(1)}, f32[128]{0:T(128)}, u32[]{:S(2)}) copy-start(f32[128]{0:T(128)} %param.13) | copy-start | bytes 1540
  18.2 7.6 %collective-permute-start.7 = (bf16[512,128]{1,0:T(8,128)(2,1)S(1)}, bf16[512,128]{1,0:T(8,128)(2,1)S(1)}, u32[]{:S(2)}, u32[]{:S(2)}) collective-permute-start(bf16[512,128]{1,0:T(8,128)(2,1)S(1)} %get-tuple-element.29), channel_id=1, source_target_pairs={{0,1},{1,0},{2,3},{3,2},{4,5},{5,4},{6,7},{7,6},{8,9},{9,8},{10,11... | collective-permute-start | bytes 393224 | tf_op jit(solution)/shard_map/ppermute | solution.py:205
  24.8 4.8 %collective-permute-start.6 = (bf16[512,128]{1,0:T(8,128)(2,1)S(1)}, bf16[512,128]{1,0:T(8,128)(2,1)S(1)}, u32[]{:S(2)}, u32[]{:S(2)}) collective-permute-start(bf16[512,128]{1,0:T(8,128)(2,1)S(1)} %get-tuple-element.27), channel_id=1, source_target_pairs={{0,1},{1,0},{2,3},{3,2},{4,5},{5,4},{6,7},{7,6},{8,9},{9,8},{10,11... | collective-permute-start | bytes 393224 | tf_op jit(solution)/shard_map/ppermute | solution.py:205
  25.3 4.3 %collective-permute-start.9 = (bf16[512,128]{1,0:T(8,128)(2,1)S(1)}, bf16[512,128]{1,0:T(8,128)(2,1)S(1)}, u32[]{:S(2)}, u32[]{:S(2)}) collective-permute-start(bf16[512,128]{1,0:T(8,128)(2,1)S(1)} %get-tuple-element.31), channel_id=1, source_target_pairs={{0,1},{1,0},{2,3},{3,2},{4,5},{5,4},{6,7},{7,6},{8,9},{9,8},{10,11... | collective-permute-start | bytes 393224 | tf_op jit(solution)/shard_map/ppermute | solution.py:205
  25.4 3.2 %collective-permute-start.10 = (bf16[512,128]{1,0:T(8,128)(2,1)S(1)}, bf16[512,128]{1,0:T(8,128)(2,1)S(1)}, u32[]{:S(2)}, u32[]{:S(2)}) collective-permute-start(bf16[512,128]{1,0:T(8,128)(2,1)S(1)} %get-tuple-element.33), channel_id=1, source_target_pairs={{0,1},{1,0},{2,3},{3,2},{4,5},{5,4},{6,7},{7,6},{8,9},{9,8},{10,11... | collective-permute-start | bytes 393224 | tf_op jit(solution)/shard_map/ppermute | solution.py:205
  25.9 12.9 %collective-permute-start.8 = (bf16[512,128]{1,0:T(8,128)(2,1)S(1)}, bf16[512,128]{1,0:T(8,128)(2,1)S(1)}, u32[]{:S(2)}, u32[]{:S(2)}) collective-permute-start(bf16[512,128]{1,0:T(8,128)(2,1)S(1)} %add_convert_fusion.1), channel_id=1, source_target_pairs={{0,8},{1,9},{2,10},{3,11},{4,12},{5,13},{6,14},{7,15},{8,0},{9,1},... | collective-permute-start | bytes 393224 | tf_op jit(solution)/shard_map/ppermute | solution.py:205
  28.6 12.2 %copy-start.3 = (bf16[128,128]{1,0:T(8,128)(2,1)S(1)}, bf16[128,128]{1,0:T(8,128)(2,1)}, u32[]{:S(2)}) copy-start(bf16[128,128]{1,0:T(8,128)(2,1)} %refs_12_.1) | copy-start | bytes 98308
  28.6 12.1 %collective-permute-start.11 = (bf16[512,128]{1,0:T(8,128)(2,1)S(1)}, bf16[512,128]{1,0:T(8,128)(2,1)S(1)}, u32[]{:S(2)}, u32[]{:S(2)}) collective-permute-start(bf16[512,128]{1,0:T(8,128)(2,1)S(1)} %add_convert_fusion), channel_id=1, source_target_pairs={{0,8},{1,9},{2,10},{3,11},{4,12},{5,13},{6,14},{7,15},{8,0},{9,1},... | collective-permute-start | bytes 393224 | tf_op jit(solution)/shard_map/ppermute | solution.py:205
  40.7 0.7 %copy-start.8 = (f32[128]{0:T(128)S(1)}, f32[128]{0:T(128)}, u32[]{:S(2)}) copy-start(f32[128]{0:T(128)} %param.16) | copy-start | bytes 1540
  40.7 0.7 %copy-start.9 = (f32[128]{0:T(128)S(1)}, f32[128]{0:T(128)}, u32[]{:S(2)}) copy-start(f32[128]{0:T(128)} %param.17) | copy-start | bytes 1540

commit v2 on v0

v2 whole, which is shorter than its diff:
```python
import functools

import jax
import jax.numpy as jnp
from jax import lax
from jax.experimental import pallas as pl
from jax.experimental.pallas import tpu as pltpu
from jax.sharding import PartitionSpec as P

SQUARE = 8
CORE, Y, Z, CORNER = 1, 2, 4, 6
FAR = (Y, Y + CORE, Z, Z + CORE, CORNER, CORNER + CORE)
F32, BF16 = jnp.float32, jnp.bfloat16

VMEM = pl.BlockSpec(memory_space=pltpu.VMEM)
SMEM = pl.BlockSpec(memory_space=pltpu.SMEM)


def dot(a, b):
    return lax.dot_general(a, b, (((1,), (0,)), ((), ())), preferred_element_type=F32)


def lane_means(x):
    lanes = x.shape[1]
    return dot(x, jnp.full((lanes, lanes), 1.0 / lanes, BF16))


def two_part_means(values):
    lanes = values.shape[1]
    high = values.astype(BF16)
    low = (values - high.astype(F32)).astype(BF16)
    ones = jnp.full((2 * lanes, lanes), 1.0 / lanes, BF16)
    return dot(jnp.concatenate([high, low], axis=1), ones)


def sigmoid(x):
    return 0.5 + 0.5 * jnp.tanh(0.5 * x)


def layer_norm(values, mean, gain, bias):
    centered = values - mean
    spread = lane_means((centered * centered).astype(BF16))
    return (centered * lax.rsqrt(spread + 1e-05) * gain + bias).astype(BF16)


def input_norm(x, gain, bias):
    return layer_norm(x.astype(F32), lane_means(x), gain, bias)


def gated(normed, w):
    half = w.shape[1] // 2
    both = dot(normed, w)
    return both[:, :half] * sigmoid(both[:, half:])


def k_valid(mask_ref, first, columns, lanes):
    at = lax.broadcasted_iota(jnp.int32, (columns, lanes), 0)
    out = jnp.zeros((columns, lanes), F32)
    for n in range(columns):
        out = jnp.where(at == n, mask_ref[first + n].astype(F32), out)
    return out


def split_weights(we_ref, wg_ref):
    half = we_ref.shape[1] // 2
    left = jnp.concatenate([we_ref[:, :half], wg_ref[:, :half]], axis=1)
    right = jnp.concatenate([we_ref[:, half:], wg_ref[:, half:]], axis=1)
    return left, right


def right_edges(normed_ref, first, rows, w, valid):
    right = gated(normed_ref[pl.ds(first, rows), :], w)
    columns, lanes = valid.shape
    return (right.reshape(rows // columns, columns, lanes) * valid).reshape(rows, lanes)


def contract(slabs, start, out, block, columns):
    at_once = 4

    def rows_of(j):
        return pl.ds(pl.multiple_of(j * block, block), block)

    def step(g, carry):
        js = [g * at_once + n for n in range(at_once)]
        sums = [None if start is None else start[rows_of(j), :] for j in js]
        for left_ref, right_ref in slabs:
            for k in range(columns):
                left = left_ref[pl.ds(k, block, stride=columns), :]
                for n, j in enumerate(js):
                    term = left * right_ref[pl.ds(j * columns + k, 1), :]
                    sums[n] = term if sums[n] is None else sums[n] + term
        for n, j in enumerate(js):
            out[rows_of(j), :] = sums[n].astype(out.dtype)
        return carry

    lax.fori_loop(0, columns // at_once, step, 0)


def block_rows(me, t, rows):
    return pl.ds(pl.multiple_of(((me // SQUARE) ^ t) * rows, rows), rows)


def edges_of(raws, lefts, rights, valids, gain, bias, weights, normed_ref, me, js, more=None):
    w_left, w_right = weights
    for m, x in enumerate(raws):
        normed = input_norm(x, gain, bias)
        normed_ref[m] = normed
        lefts[m][...] = gated(normed, w_left)
        if more is not None:
            more(m, normed)
    for m in range(len(raws)):
        first = pl.multiple_of((me % SQUARE) * js, js)
        rights[m][...] = right_edges(normed_ref.at[m], first, js, w_right, valids[m])


def own_kernel(squares, block, columns, *refs):
    me_ref, mask_ref, mask_row_ref, *refs = refs
    slabs, refs = refs[:2], refs[2:]
    gain_ref, bias_ref, we_ref, wg_ref, gate_ref, w_out_ref, out_gain_ref, out_bias_ref, *refs = refs
    gates_ref, far_valid_ref, i_valid_ref, j_valid_ref, w_copy_ref, norm_copy_ref, *refs = refs
    lefts, refs = refs[: 2 * squares], refs[2 * squares :]
    rights, refs = refs[: 2 * squares], refs[2 * squares :]
    shares, (normed_ref,) = refs[:-1], refs[-1:]
    me = me_ref[0]
    lanes = gates_ref.shape[1]
    rows, js = block * columns, columns * columns
    residues = mask_row_ref.shape[1]
    valids = [k_valid(mask_ref, (me ^ b) * columns, columns, lanes) for b in (0, CORE)]

    def gates(m, normed):
        if m < squares:
            gates_ref[m * rows : (m + 1) * rows, :] = sigmoid(dot(normed, gate_ref[...]))

    edges_of(
        [slab[block_rows(me, t, rows), :] for slab in slabs for t in range(squares)],
        lefts, rights, [valids[0]] * squares + [valids[1]] * squares,
        gain_ref[...], bias_ref[...], split_weights(we_ref, wg_ref), normed_ref, me, js, gates,
    )
    for t in range(squares):
        for s in range(1, squares):
            terms = [(lefts[t], rights[s]), (lefts[squares + t], rights[squares + s])]
            contract(terms, None, shares[t * (squares - 1) + s - 1], block, columns)
    for n, bits in enumerate(FAR):
        far_valid_ref[n * columns : (n + 1) * columns, :] = k_valid(mask_ref, (me ^ bits) * columns, columns, lanes)
    j_valid_ref[...] = valids[0]
    for t in range(squares):
        at = lax.broadcasted_iota(jnp.int32, (block, residues), 0) + ((me // SQUARE) ^ t) * block
        chosen = jnp.where(lax.broadcasted_iota(jnp.int32, (block, residues), 1) == at, mask_row_ref[...], 0)
        i_valid_ref[t * block : (t + 1) * block, :] = dot(chosen.astype(F32).astype(BF16), jnp.ones((residues, lanes), BF16))
    w_copy_ref[...] = w_out_ref[...]
    norm_copy_ref[:1, :] = out_gain_ref[...]
    norm_copy_ref[1:, :] = out_bias_ref[...]


def piece_kernel(new, old, products, block, columns, *refs):
    refs = list(refs)

    def take(n):
        out = refs[:n]
        del refs[:n]
        return out

    rows, js = block * columns, columns * columns
    if new:
        me = take(1)[0][0]
        raw = take(len(new))
        valid_ref, gain_ref, bias_ref, we_ref, wg_ref = take(5)
    old_lefts, old_rights = take(len(old)), take(len(old))
    starts = [take(1)[0] if begun else None for _, _, begun in products]
    new_lefts, new_rights = take(len(new)), take(len(new))
    outs = take(len(products))
    edges = dict(zip(old, zip(old_lefts, old_rights)))
    if new:
        edges_of(
            [x[block_rows(me, t, rows) if x.shape[0] > rows else pl.ds(0, rows), :] for x, (_, t) in zip(raw, new)],
            new_lefts, new_rights, [valid_ref[pl.ds(FAR.index(b) * columns, columns), :] for b, _ in new],
            gain_ref[...], bias_ref[...], split_weights(we_ref, wg_ref), refs[0], me, js,
        )
        edges.update(zip(new, zip(new_lefts, new_rights)))
    for ((t, s), slabs, _), start, out in zip(products, starts, outs):
        contract([(edges[b, t][0], edges[b, s][1]) for b in slabs], start, out, block, columns)


def last_kernel(t, n_sums, block, columns, me_ref, *refs):
    i_valid_ref, j_valid_ref, *refs = refs
    sums, refs = refs[:n_sums], refs[n_sums:]
    gates_ref, norm_ref, w_ref, *refs = refs
    out_ref, turned_ref = refs[-2:]
    rows = block * columns
    outer = sums[0][...]
    for other in sums[1:]:
        outer = outer + other[...].astype(F32)
    i_valid = i_valid_ref[t * block : (t + 1) * block, :]
    outer = outer * jnp.concatenate([i_valid * j_valid_ref[j : j + 1, :] for j in range(columns)], axis=0)
    normed = layer_norm(outer, two_part_means(outer), norm_ref[:1, :], norm_ref[1:, :])
    projected = dot(normed, w_ref[...])
    for j in range(columns):
        turned_ref[pl.ds(j, block, stride=columns), :] = projected[j * block : (j + 1) * block, :]
    out_ref[...] = (turned_ref[...] * gates_ref[t * rows : (t + 1) * rows, :]).astype(BF16)


def call(kernel, operands, smem, outs, scratch=()):
    return pl.pallas_call(
        kernel,
        out_shape=[jax.ShapeDtypeStruct(shape, dtype) for shape, dtype in outs],
        in_specs=[SMEM] * smem + [VMEM] * (len(operands) - smem),
        out_specs=[VMEM] * len(outs),
        scratch_shapes=list(scratch),
        compiler_params=pltpu.CompilerParams(vmem_limit_bytes=12 << 20),
    )(*operands)


def local(size, pair, residue_mask, ln_in_gain, ln_in_bias, w_edges, w_edge_gates, ln_out_gain, ln_out_bias, w_gate, w_out):
    residues, columns, lanes = pair.shape
    squares = size // SQUARE
    block = residues // squares
    rows, js = block * columns, columns * columns
    index = lax.axis_index("row")
    me = index.astype(jnp.int32).reshape(1)
    square = index // SQUARE

    def swap(value, bits):
        return lax.ppermute(value, "row", [(i, i ^ bits) for i in range(size)])

    in_gain, in_bias = ln_in_gain.reshape(1, lanes), ln_in_bias.reshape(1, lanes)
    flat = pair.reshape(residues * columns, lanes)
    order = list(range(1, squares)) + [0]
    raw = {}
    whole = swap(flat, CORNER)
    for t in order:
        own = lax.dynamic_slice_in_dim(pair, (square ^ t) * block, block, 0).reshape(rows, lanes)
        for b in (Z, Y):
            raw[b, t] = swap(own, b)
    near_whole = swap(flat, CORE)

    tile = lambda n, dtype=F32: ((n, lanes), dtype)
    with jax.named_scope("own_slab"):
        gates, far_valid, i_valid, j_valid, w_last, norm_last, *made = call(
            functools.partial(own_kernel, squares, block, columns),
            (me, residue_mask, residue_mask.reshape(1, residues), flat, near_whole, in_gain, in_bias, w_edges, w_edge_gates)
            + (w_gate, w_out, ln_out_gain.reshape(1, lanes), ln_out_bias.reshape(1, lanes)),
            2,
            [tile(squares * rows), tile(len(FAR) * columns), tile(squares * block), tile(columns), tile(lanes, BF16), tile(2)]
            + [tile(rows)] * (2 * squares) + [tile(js)] * (2 * squares) + [tile(rows)] * (squares * (squares - 1)),
            [pltpu.VMEM((2 * squares, rows, lanes), BF16)],
        )
    near = [(b, t) for b in (0, CORE) for t in range(squares)]
    lefts = dict(zip(near, made))
    rights = dict(zip(near, made[2 * squares :]))
    others = [(t, s) for t in range(squares) for s in range(1, squares)]
    sums = dict(zip(others, made[4 * squares :]))

    def pieces(new, products):
        read = sorted({(b, u) for (t, s), slabs, *_ in products for b in slabs for u in (t, s)} - set(new))
        operands = []
        if new:
            operands += [me] + [raw[p] for p in new] + [far_valid, in_gain, in_bias, w_edges, w_edge_gates]
        operands += [lefts[p] for p in read] + [rights[p] for p in read] + [sums[ts] for ts, _, begun, _ in products if begun]
        made = call(
            functools.partial(piece_kernel, tuple(new), tuple(read), tuple(p[:3] for p in products), block, columns),
            operands,
            1 if new else 0,
            [tile(rows)] * len(new) + [tile(js)] * len(new) + [tile(rows, dtype) for *_, dtype in products],
            [pltpu.VMEM((len(new), rows, lanes), BF16)] if new else [],
        )
        for n, p in enumerate(new):
            lefts[p], rights[p] = made[n], made[len(new) + n]
        return made[2 * len(new) :]

    def hand_on(names, after):
        for b, ts in names:
            value, _ = lax.optimization_barrier((raw[b, ts[0]], after))
            value = swap(value, CORE)
            raw.update({(b + CORE, t): value for t in ts})

    first, rest = order[0], order[1:]
    raw.update({(CORNER, t): whole for t in order})
    missing = {ts: set(FAR) for ts in others}
    arrived = {}

    def work(step):
        have = set(lefts) | set(step)
        products = []
        for (t, s), slabs in missing.items():
            now = tuple(b for b in FAR if b in slabs and (b, t) in have and (b, s) in have)
            if now:
                slabs -= set(now)
                products.append(((t, s), now, True, F32 if slabs else BF16))
        with jax.named_scope("pieces"):
            made = pieces(step, products)
        for ((t, s), *_, dtype), value in zip(products, made):
            if dtype == F32:
                sums[t, s] = value
            else:
                arrived[t ^ s, s] = swap(value, SQUARE * s)
        return lefts[step[0]]

    hand_on([(Z, [first])], gates)
    after = work([(Z, first)])
    hand_on([(Y, [first]), (CORNER, order)], after)
    after = work([(Y, first), (CORNER, first), (Z + CORE, first)])
    for t in rest:
        hand_on([(Z, [t]), (Y, [t])], after)
    work([(Y + CORE, first), (CORNER + CORE, first)])
    for t in rest:
        work([(b, t) for b in FAR])
    with jax.named_scope("own_outer"):
        own_sums = pieces([], [((t, 0), (0, CORE, *FAR), False, F32) for t in range(squares)])

    update = None
    for t in range(squares):
        others = [arrived[t, s] for s in range(1, squares)]
        before = () if update is None else (update,)
        operands = (me, i_valid, j_valid, own_sums[t], *others, gates, norm_last, w_last, *before)
        with jax.named_scope("update"):
            update = pl.pallas_call(
                functools.partial(last_kernel, t, 1 + len(others), block, columns),
                out_shape=jax.ShapeDtypeStruct((residues * columns, lanes), BF16),
                grid_spec=pltpu.PrefetchScalarGridSpec(
                    num_scalar_prefetch=1,
                    grid=(1,),
                    in_specs=[VMEM] * (6 + len(others)) + [pl.BlockSpec(memory_space=pl.ANY)] * len(before),
                    out_specs=pl.BlockSpec((rows, lanes), lambda i, me_ref, t=t: ((me_ref[0] // SQUARE) ^ t, 0)),
                    scratch_shapes=[pltpu.VMEM((rows, lanes), F32)],
                ),
                input_output_aliases={len(operands) - 1: 0} if before else {},
                compiler_params=pltpu.CompilerParams(vmem_limit_bytes=12 << 20),
            )(*operands)
    return update.reshape(residues, columns, lanes)


def solution(mesh):
    return jax.shard_map(
        functools.partial(local, mesh.shape["row"]),
        mesh=mesh,
        in_specs=(P("groups", "row", None), P("groups"), P(), P(), P(), P(), P(), P(), P(), P()),
        out_specs=P("groups", "row", None),
        check_vma=False,
    )
```

time: 89.7 us -> 35.8 us (0.40)
  waiting for transfers between devices: 47.7 us -> 6.72 us
  Pallas kernels: 0 us -> 14.7 us
  between operations: 13.5 us -> 0.14 us
  local copies, waits for them, and re-layouts: 9.97 us -> 1.72 us
  matrix products: 5.51 us -> 0 us
  other arithmetic: 5.06 us -> 0 us
  starting transfers between devices: 7.4 us -> 12.4 us
    all_gather x1 -> x0, waiting for transfers between devices: 35.7 us -> none  [local(): lax.all_gather(left, 'row', axis=1, tiled=True)]
    pallas_call x0 -> x8, Pallas kernels: none -> 14.7 us  [the longest x6 12.3 us: call(): pl.pallas_call(kernel, out_shape=[jax.ShapeDtypeStruct(shape, dtype) for...]
    ppermute x0 -> x13, starting transfers between devices: none -> 12.4 us  [swap(): return lax.ppermute(value, 'row', [(i, i ^ bits) for i in range(size)])]
    all_to_all x1 -> x0, waiting for transfers between devices: 12 us -> none  [local(): lax.all_to_all(right, 'row', split_axis=0, concat_axis=1, tiled=True)]
    all_to_all x1 -> x0, starting transfers between devices: 7.4 us -> none  [local(): lax.all_to_all(right, 'row', split_axis=0, concat_axis=1, tiled=True)]
    all_gather x1 -> x0, local copies, waits for them, and re-layouts: 6.74 us -> none  [local(): lax.all_gather(left, 'row', axis=1, tiled=True)]
    ppermute x0 -> x13, waiting for transfers between devices: none -> 6.72 us  [swap(): return lax.ppermute(value, 'row', [(i, i ^ bits) for i in range(size)])]
    dot_general x5 -> x0, matrix products: 5.51 us -> none  [the longest x1 3.41 us: local(): jnp.einsum('ikc,jkc->ijc', lax.all_gather(left, 'row', axis=1, tiled=True...]
  transfers between devices with their start and end apart: 2 -> 13, of which waited for: 2 -> 3; matrix products, arithmetic and copies ran while one was open for 2% -> 3% of each run, Pallas kernels for 0% -> 38%
where the time goes in v2:
time: 35.8 us; the launch traced here: 35.7 us
  Pallas kernels  14.7 us (41%)
  starting transfers between devices  12.4 us (35%)
  waiting for transfers between devices  6.72 us (19%)
  local copies, waits for them, and re-layouts  1.72 us (5%)
    ppermute x13, starting transfers between devices, swap(): return lax.ppermute(value, 'row', [(i, i ^ bits) for i in range(size)])  12.4 us
    pallas_call x6, Pallas kernels, call(): pl.pallas_call(kernel, out_shape=[jax.ShapeDtypeStruct(shape, dtype) for...  12.3 us
    ppermute x13, waiting for transfers between devices, swap(): return lax.ppermute(value, 'row', [(i, i ^ bits) for i in range(size)])  6.72 us
    pallas_call x2, Pallas kernels, local(): pl.pallas_call(functools.partial(last_kernel, t, 1 + len(others), block,...  2.4 us
    reshape x1, local copies, waits for them, and re-layouts, local(): lax.dynamic_slice_in_dim(pair, (square ^ t) * block, block, 0)  1.05 us
  transfers between devices with their start and end apart: 13, of which 3 were waited for; matrix products, arithmetic and copies ran while one was open for 3% of the time, Pallas kernels for 38%

profile of v2, /device:TPU:0, one launch (start us, length us, event | category | flops | bytes accessed | tf_op | source)
XLA Modules:
  0.0 35.7 jit_solution(2762784914430495587)
XLA Ops:
  0.0 0.5 %collective-permute-start = (bf16[1024,128]{1,0:T(8,128)(2,1)}, bf16[1024,128]{1,0:T(8,128)(2,1)S(1)}, u32[]{:S(2)}, u32[]{:S(2)}) collective-permute-start(bf16[1024,128]{1,0:T(8,128)(2,1)} %bitcast.12), channel_id=1, source_target_pairs={{0,1},{1,0},{2,3},{3,2},{4,5},{5,4},{6,7},{7,6},{8,9},{9,8},{10,11... | collective-permute-start | bytes 786440 | tf_op jit(solution)/shard_map/ppermute | solution.py:223
  0.5 3.5 %collective-permute-start.3 = (bf16[1024,128]{1,0:T(8,128)(2,1)}, bf16[1024,128]{1,0:T(8,128)(2,1)S(1)}, u32[]{:S(2)}, u32[]{:S(2)}) collective-permute-start(bf16[1024,128]{1,0:T(8,128)(2,1)} %bitcast.13), channel_id=1, source_target_pairs={{0,6},{1,7},{2,4},{3,5},{4,2},{5,3},{6,0},{7,1},{8,14},{9,15},{10,... | collective-permute-start | bytes 786440 | tf_op jit(solution)/shard_map/ppermute | solution.py:223
  4.0 1.0 %dynamic-slice_bitcast_fusion = (bf16[512,128]{1,0:T(8,128)(2,1)S(1)}, bf16[512,128]{1,0:T(8,128)(2,1)S(1)}) fusion(bf16[128,8,128]{2,1,0:T(8,128)(2,1)} %param.10, s32[]{:T(128)S(6)} %select_n.13, s32[]{:T(128)S(6)} %select_n.12), kind=kLoop, calls=%fused_computation | loop fusion | bytes 524296 | tf_op jit(solution)/shard_map/reshape | solution.py:231
  5.1 0.5 %collective-permute-start.4 = (bf16[512,128]{1,0:T(8,128)(2,1)S(1)}, bf16[512,128]{1,0:T(8,128)(2,1)S(1)}, u32[]{:S(2)}, u32[]{:S(2)}) collective-permute-start(bf16[512,128]{1,0:T(8,128)(2,1)S(1)} %get-tuple-element.107), channel_id=1, source_target_pairs={{0,4},{1,5},{2,6},{3,7},{4,0},{5,1},{6,2},{7,3},{8,12},{9,13},{10,... | collective-permute-start | bytes 393224 | tf_op jit(solution)/shard_map/ppermute | solution.py:223
  5.6 0.2 collective-permute-start.2
  5.7 1.9 %collective-permute-start.7 = (bf16[512,128]{1,0:T(8,128)(2,1)S(1)}, bf16[512,128]{1,0:T(8,128)(2,1)S(1)}, u32[]{:S(2)}, u32[]{:S(2)}) collective-permute-start(bf16[512,128]{1,0:T(8,128)(2,1)S(1)} %get-tuple-element.108), channel_id=1, source_target_pairs={{0,4},{1,5},{2,6},{3,7},{4,0},{5,1},{6,2},{7,3},{8,12},{9,13},{10,... | collective-permute-start | bytes 393224 | tf_op jit(solution)/shard_map/ppermute | solution.py:223
  7.7 1.5 %collective-permute-start.1 = (bf16[512,128]{1,0:T(8,128)(2,1)S(1)}, bf16[512,128]{1,0:T(8,128)(2,1)S(1)}, u32[]{:S(2)}, u32[]{:S(2)}) collective-permute-start(bf16[512,128]{1,0:T(8,128)(2,1)S(1)} %get-tuple-element.108), channel_id=1, source_target_pairs={{0,2},{1,3},{2,0},{3,1},{4,6},{5,7},{6,4},{7,5},{8,10},{9,11},{10,... | collective-permute-start | bytes 393224 | tf_op jit(solution)/shard_map/ppermute | solution.py:223
  9.3 0.6 %copy-done.8 = f32[128]{0:T(128)S(1)} copy-done((f32[128]{0:T(128)S(1)}, f32[128]{0:T(128)}, u32[]{:S(2)}) %copy-start.8) | copy-done | bytes 536
  9.9 3.0 %own_slab.1 = (f32[1024,128]{1,0:T(8,128)S(1)}, f32[48,128]{1,0:T(8,128)S(1)}, f32[128,128]{1,0:T(8,128)S(1)}, f32[8,128]{1,0:T(8,128)S(1)}, bf16[128,128]{1,0:T...) custom-call(s32[1]{0:T(128)} %bitcast.refs_0_.me_ref, ...), custom_call_target="tpu_custom_call" | custom-call | tf_op jit(solution)/shard_map/own_slab/pallas_call | solution.py:203
  12.9 1.7 %collective-permute-done.4.refs_1_ = bf16[512,128]{1,0:T(8,128)(2,1)S(1)} collective-permute-done((bf16[512,128]{1,0:T(8,128)(2,1)S(1)}, bf16[512,128]{1,0:T(8,128)(2,1)S(1)}, u32[]{:S(2)}, u32[]{:S(2)}) %collective-permute-start.4) | collective-permute-done | bytes 131104 | tf_op jit(solution)/shard_map/ppermute | solution.py:223
  14.6 0.7 %pieces.4 = (f32[512,128]{1,0:T(8,128)S(1)}, f32[64,128]{1,0:T(8,128)S(1)}, f32[512,128]{1,0:T(8,128)S(1)}) custom-call(s32[1]{0:T(128)} %bitcast.refs_0_.me_ref, bf16[512,128]{1,0:T(8,128)(2,1)S(1)} %collective-permute-done.4.refs_1_, f32[48,128]{1,0:T(8,128)S(1)} %get-tuple-element.64.refs_2_.refs_4_.refs_3_.refs_7_, f32[1,128]{1,0:T(1,128)S(1)} %bitcast.16, ...), custom_call_target="tpu_custom_call" | custom-call | tf_op jit(solution)/shard_map/pieces/pallas_call | solution.py:203
  15.3 0.6 %collective-permute-start.9 = (bf16[1024,128]{1,0:T(8,128)(2,1)S(1)}, bf16[1024,128]{1,0:T(8,128)(2,1)S(1)}, u32[]{:S(2)}, u32[]{:S(2)}) collective-permute-start(bf16[1024,128]{1,0:T(8,128)(2,1)S(1)} %collective-permute-done.3.refs_2_.refs_5_), channel_id=1, source_target_pairs={{0,1},{1,0},{2,3},{3,2},{4,5},{5,4},{6,7},{7,6},{8,9},{9,8},{10,11... | collective-permute-start | bytes 786440 | tf_op jit(solution)/shard_map/ppermute | solution.py:223
  15.9 0.1 collective-permute-start.10
  16.0 1.5 %pieces.5 = (f32[512,128]{1,0:T(8,128)S(1)}, f32[512,128]{1,0:T(8,128)S(1)}, f32[512,128]{1,0:T(8,128)S(1)}, f32[64,128]{1,0:T(8,128)S(1)}, f32[64,128]{1,0:T(8,...) custom-call(s32[1]{0:T(128)} %bitcast.refs_0_.me_ref, bf16[512,128]{1,0:T(8,128)(2,1)S(1)} %collective-permute-done.2.refs_1_, ...), custom_call_target="tpu_custom_call" | custom-call | tf_op jit(solution)/shard_map/pieces/pallas_call | solution.py:203
  17.6 0.5 %collective-permute-start.6 = (bf16[512,128]{1,0:T(8,128)(2,1)S(1)}, bf16[512,128]{1,0:T(8,128)(2,1)S(1)}, u32[]{:S(2)}, u32[]{:S(2)}) collective-permute-start(bf16[512,128]{1,0:T(8,128)(2,1)S(1)} %collective-permute-done.1.refs_1_), channel_id=1, source_target_pairs={{0,1},{1,0},{2,3},{3,2},{4,5},{5,4},{6,7},{7,6},{8,9},{9,8},{10,11... | collective-permute-start | bytes 393224 | tf_op jit(solution)/shard_map/ppermute | solution.py:223
  18.1 1.1 %pieces.6 = (f32[512,128]{1,0:T(8,128)S(1)}, f32[512,128]{1,0:T(8,128)S(1)}, f32[64,128]{1,0:T(8,128)S(1)}, f32[64,128]{1,0:T(8,128)S(1)}, bf16[512,128]{1,0:T(8,128)(2,1)S(1)}) custom-call(s32[1]{0:T(128)} %bitcast.refs_0_.me_ref, bf16[512,128]{1,0:T(8,128)(2,1)S(1)} %collective-permute-done.10.refs_1_, ...), custom_call_target="tpu_custom_call" | custom-call | tf_op jit(solution)/shard_map/pieces/pallas_call | solution.py:203
  19.2 2.7 %collective-permute-start.12 = (bf16[512,128]{1,0:T(8,128)(2,1)S(1)}, bf16[512,128]{1,0:T(8,128)(2,1)S(1)}, u32[]{:S(2)}, u32[]{:S(2)}) collective-permute-start(bf16[512,128]{1,0:T(8,128)(2,1)S(1)} %get-tuple-element.106), channel_id=1, source_target_pairs={{0,8},{1,9},{2,10},{3,11},{4,12},{5,13},{6,14},{7,15},{8,0},{9,1},... | collective-permute-start | bytes 393224 | tf_op jit(solution)/shard_map/ppermute | solution.py:223
  21.9 2.6 %pieces.7 = (f32[512,128]{1,0:T(8,128)S(1)}, f32[512,128]{1,0:T(8,128)S(1)}, f32[512,128]{1,0:T(8,128)S(1)}, f32[512,128]{1,0:T(8,128)S(1)}, f32[512,128]{1,0:T(...) custom-call(s32[1]{0:T(128)} %bitcast.refs_0_.me_ref, ...), custom_call_target="tpu_custom_call" | custom-call | tf_op jit(solution)/shard_map/pieces/pallas_call | solution.py:203
  24.5 0.4 %collective-permute-start.11 = (bf16[512,128]{1,0:T(8,128)(2,1)S(1)}, bf16[512,128]{1,0:T(8,128)(2,1)S(1)}, u32[]{:S(2)}, u32[]{:S(2)}) collective-permute-start(bf16[512,128]{1,0:T(8,128)(2,1)S(1)} %get-tuple-element.102), channel_id=1, source_target_pairs={{0,8},{1,9},{2,10},{3,11},{4,12},{5,13},{6,14},{7,15},{8,0},{9,1},... | collective-permute-start | bytes 393224 | tf_op jit(solution)/shard_map/ppermute | solution.py:223
  24.9 3.4 %own_outer.1 = (f32[512,128]{1,0:T(8,128)S(1)}, f32[512,128]{1,0:T(8,128)S(1)}) custom-call(f32[512,128]{1,0:T(8,128)S(1)} %get-tuple-element.58.refs_0_, f32[512,128]{1,0:T(8,128)S(1)} %get-tuple-element.59.refs_1_, f32[512,128]{1,0:T(8,128)S(1)} %get-tuple-element.60.refs_2_, f32[512,128]{1,0:T(8,128)S(1)} %get-tuple-element.61.refs_3_, ...), custom_call_target="tpu_custom_call" | custom-call | tf_op jit(solution)/shard_map/own_outer/pallas_call | solution.py:203
  28.3 3.8 %collective-permute-done.12.refs_3_ = bf16[512,128]{1,0:T(8,128)(2,1)S(1)} collective-permute-done((bf16[512,128]{1,0:T(8,128)(2,1)S(1)}, bf16[512,128]{1,0:T(8,128)(2,1)S(1)}, u32[]{:S(2)}, u32[]{:S(2)}) %collective-permute-start.12) | collective-permute-done | bytes 131104 | tf_op jit(solution)/shard_map/ppermute | solution.py:223
  32.1 1.2 %update.2.refs_7_ = bf16[1024,128]{1,0:T(8,128)(2,1)} custom-call(s32[1]{0:T(128)} %bitcast.refs_0_.me_ref, f32[128,128]{1,0:T(8,128)S(1)} %get-tuple-element.56.refs_0_, f32[8,128]{1,0:T(8,128)S(1)} %get-tuple-element.57.refs_1_, f32[512,128]{1,0:T(8,128)S(1)} %get-tuple-element.105.refs_2_, bf16[512,128]{1,0:T(8,128)(2,1)S(1)} %collective-permute-done.12.refs_3_, ...), custom_call_target="tpu_custom_call" | custom-call | tf_op jit(solution)/shard_map/update/pallas_call | solution.py:316
  33.3 1.1 %collective-permute-done.11.refs_3_ = bf16[512,128]{1,0:T(8,128)(2,1)S(1)} collective-permute-done((bf16[512,128]{1,0:T(8,128)(2,1)S(1)}, bf16[512,128]{1,0:T(8,128)(2,1)S(1)}, u32[]{:S(2)}, u32[]{:S(2)}) %collective-permute-start.11) | collective-permute-done | bytes 131104 | tf_op jit(solution)/shard_map/ppermute | solution.py:223
  34.5 1.2 %update.3 = bf16[1024,128]{1,0:T(8,128)(2,1)} custom-call(s32[1]{0:T(128)} %bitcast.refs_0_.me_ref, f32[128,128]{1,0:T(8,128)S(1)} %get-tuple-element.56.refs_0_, f32[8,128]{1,0:T(8,128)S(1)} %get-tuple-element.57.refs_1_, f32[512,128]{1,0:T(8,128)S(1)} %get-tuple-element.101.refs_2_, ...), custom_call_target="tpu_custom_call", output_to_operand_aliasing={{}: (8, {})} | custom-call | tf_op jit(solution)/shard_map/update/pallas_call | solution.py:316
  (31 shorter events, 0.2 us)
Async XLA Ops:
  0.0 7.7 %collective-permute-start = (bf16[1024,128]{1,0:T(8,128)(2,1)}, bf16[1024,128]{1,0:T(8,128)(2,1)S(1)}, u32[]{:S(2)}, u32[]{:S(2)}) collective-permute-start(bf16[1024,128]{1,0:T(8,128)(2,1)} %bitcast.12), channel_id=1, source_target_pairs={{0,1},{1,0},{2,3},{3,2},{4,5},{5,4},{6,7},{7,6},{8,9},{9,8},{10,11... | collective-permute-start | bytes 786440 | tf_op jit(solution)/shard_map/ppermute | solution.py:223
  0.5 14.9 %collective-permute-start.3 = (bf16[1024,128]{1,0:T(8,128)(2,1)}, bf16[1024,128]{1,0:T(8,128)(2,1)S(1)}, u32[]{:S(2)}, u32[]{:S(2)}) collective-permute-start(bf16[1024,128]{1,0:T(8,128)(2,1)} %bitcast.13), channel_id=1, source_target_pairs={{0,6},{1,7},{2,4},{3,5},{4,2},{5,3},{6,0},{7,1},{8,14},{9,15},{10,... | collective-permute-start | bytes 786440 | tf_op jit(solution)/shard_map/ppermute | solution.py:223
  4.0 5.2 %copy-start = (bf16[128,256]{1,0:T(8,128)(2,1)S(1)}, bf16[128,256]{1,0:T(8,128)(2,1)}, u32[]{:S(2)}) copy-start(bf16[128,256]{1,0:T(8,128)(2,1)} %refs_10_.3) | copy-start | bytes 196612
  4.0 5.2 %copy-start.1 = (bf16[128,256]{1,0:T(8,128)(2,1)S(1)}, bf16[128,256]{1,0:T(8,128)(2,1)}, u32[]{:S(2)}) copy-start(bf16[128,256]{1,0:T(8,128)(2,1)} %refs_11_.1) | copy-start | bytes 196612
  4.0 5.2 %copy-start.2 = (bf16[128,8,128]{2,1,0:T(8,128)(2,1)S(1)}, bf16[128,8,128]{2,1,0:T(8,128)(2,1)}, u32[]{:S(2)}) copy-start(bf16[128,8,128]{2,1,0:T(8,128)(2,1)} %param.10) | copy-start | bytes 786436
  4.0 5.2 %copy-start.3 = (bf16[128,128]{1,0:T(8,128)(2,1)S(1)}, bf16[128,128]{1,0:T(8,128)(2,1)}, u32[]{:S(2)}) copy-start(bf16[128,128]{1,0:T(8,128)(2,1)} %refs_9_.1) | copy-start | bytes 98308
  4.0 5.2 %copy-start.4 = (bf16[128,128]{1,0:T(8,128)(2,1)S(1)}, bf16[128,128]{1,0:T(8,128)(2,1)}, u32[]{:S(2)}) copy-start(bf16[128,128]{1,0:T(8,128)(2,1)} %refs_10_.2) | copy-start | bytes 98308
  5.1 9.5 %collective-permute-start.4 = (bf16[512,128]{1,0:T(8,128)(2,1)S(1)}, bf16[512,128]{1,0:T(8,128)(2,1)S(1)}, u32[]{:S(2)}, u32[]{:S(2)}) collective-permute-start(bf16[512,128]{1,0:T(8,128)(2,1)S(1)} %get-tuple-element.107), channel_id=1, source_target_pairs={{0,4},{1,5},{2,6},{3,7},{4,0},{5,1},{6,2},{7,3},{8,12},{9,13},{10,... | collective-permute-start | bytes 393224 | tf_op jit(solution)/shard_map/ppermute | solution.py:223
  5.6 10.3 %collective-permute-start.2 = (bf16[512,128]{1,0:T(8,128)(2,1)S(1)}, bf16[512,128]{1,0:T(8,128)(2,1)S(1)}, u32[]{:S(2)}, u32[]{:S(2)}) collective-permute-start(bf16[512,128]{1,0:T(8,128)(2,1)S(1)} %get-tuple-element.107), channel_id=1, source_target_pairs={{0,2},{1,3},{2,0},{3,1},{4,6},{5,7},{6,4},{7,5},{8,10},{9,11},{10,... | collective-permute-start | bytes 393224 | tf_op jit(solution)/shard_map/ppermute | solution.py:223
  5.7 11.8 %collective-permute-start.7 = (bf16[512,128]{1,0:T(8,128)(2,1)S(1)}, bf16[512,128]{1,0:T(8,128)(2,1)S(1)}, u32[]{:S(2)}, u32[]{:S(2)}) collective-permute-start(bf16[512,128]{1,0:T(8,128)(2,1)S(1)} %get-tuple-element.108), channel_id=1, source_target_pairs={{0,4},{1,5},{2,6},{3,7},{4,0},{5,1},{6,2},{7,3},{8,12},{9,13},{10,... | collective-permute-start | bytes 393224 | tf_op jit(solution)/shard_map/ppermute | solution.py:223
  7.7 9.9 %collective-permute-start.1 = (bf16[512,128]{1,0:T(8,128)(2,1)S(1)}, bf16[512,128]{1,0:T(8,128)(2,1)S(1)}, u32[]{:S(2)}, u32[]{:S(2)}) collective-permute-start(bf16[512,128]{1,0:T(8,128)(2,1)S(1)} %get-tuple-element.108), channel_id=1, source_target_pairs={{0,2},{1,3},{2,0},{3,1},{4,6},{5,7},{6,4},{7,5},{8,10},{9,11},{10,... | collective-permute-start | bytes 393224 | tf_op jit(solution)/shard_map/ppermute | solution.py:223
  9.2 0.7 %copy-start.8 = (f32[128]{0:T(128)S(1)}, f32[128]{0:T(128)}, u32[]{:S(2)}) copy-start(f32[128]{0:T(128)} %param.16) | copy-start | bytes 1540
  9.2 0.7 %copy-start.9 = (f32[128]{0:T(128)S(1)}, f32[128]{0:T(128)}, u32[]{:S(2)}) copy-start(f32[128]{0:T(128)} %param.17) | copy-start | bytes 1540
  9.2 0.7 %copy-start.5 = (f32[128]{0:T(128)S(1)}, f32[128]{0:T(128)}, u32[]{:S(2)}) copy-start(f32[128]{0:T(128)} %param.12) | copy-start | bytes 1540
  9.2 0.7 %copy-start.6 = (f32[128]{0:T(128)S(1)}, f32[128]{0:T(128)}, u32[]{:S(2)}) copy-start(f32[128]{0:T(128)} %param.13) | copy-start | bytes 1540
  9.2 0.7 %copy-start.7 = (s32[128]{0:T(128)S(1)}, s32[128]{0:T(128)}, u32[]{:S(2)}) copy-start(s32[128]{0:T(128)} %refs_1_.1) | copy-start | bytes 1540
  14.6 1.4 %collective-permute-start.5 = (bf16[512,128]{1,0:T(8,128)(2,1)S(1)}, bf16[512,128]{1,0:T(8,128)(2,1)S(1)}, u32[]{:S(2)}, u32[]{:S(2)}) collective-permute-start(bf16[512,128]{1,0:T(8,128)(2,1)S(1)} %collective-permute-done.4.refs_1_), channel_id=1, source_target_pairs={{0,1},{1,0},{2,3},{3,2},{4,5},{5,4},{6,7},{7,6},{8,9},{9,8},{10,11... | collective-permute-start | bytes 393224 | tf_op jit(solution)/shard_map/ppermute | solution.py:223
  15.3 2.8 %collective-permute-start.9 = (bf16[1024,128]{1,0:T(8,128)(2,1)S(1)}, bf16[1024,128]{1,0:T(8,128)(2,1)S(1)}, u32[]{:S(2)}, u32[]{:S(2)}) collective-permute-start(bf16[1024,128]{1,0:T(8,128)(2,1)S(1)} %collective-permute-done.3.refs_2_.refs_5_), channel_id=1, source_target_pairs={{0,1},{1,0},{2,3},{3,2},{4,5},{5,4},{6,7},{7,6},{8,9},{9,8},{10,11... | collective-permute-start | bytes 786440 | tf_op jit(solution)/shard_map/ppermute | solution.py:223
  15.9 2.2 %collective-permute-start.10 = (bf16[512,128]{1,0:T(8,128)(2,1)S(1)}, bf16[512,128]{1,0:T(8,128)(2,1)S(1)}, u32[]{:S(2)}, u32[]{:S(2)}) collective-permute-start(bf16[512,128]{1,0:T(8,128)(2,1)S(1)} %collective-permute-done.2.refs_1_), channel_id=1, source_target_pairs={{0,1},{1,0},{2,3},{3,2},{4,5},{5,4},{6,7},{7,6},{8,9},{9,8},{10,11... | collective-permute-start | bytes 393224 | tf_op jit(solution)/shard_map/ppermute | solution.py:223
  17.6 4.3 %collective-permute-start.6 = (bf16[512,128]{1,0:T(8,128)(2,1)S(1)}, bf16[512,128]{1,0:T(8,128)(2,1)S(1)}, u32[]{:S(2)}, u32[]{:S(2)}) collective-permute-start(bf16[512,128]{1,0:T(8,128)(2,1)S(1)} %collective-permute-done.1.refs_1_), channel_id=1, source_target_pairs={{0,1},{1,0},{2,3},{3,2},{4,5},{5,4},{6,7},{7,6},{8,9},{9,8},{10,11... | collective-permute-start | bytes 393224 | tf_op jit(solution)/shard_map/ppermute | solution.py:223
  18.0 3.8 %collective-permute-start.8 = (bf16[512,128]{1,0:T(8,128)(2,1)S(1)}, bf16[512,128]{1,0:T(8,128)(2,1)S(1)}, u32[]{:S(2)}, u32[]{:S(2)}) collective-permute-start(bf16[512,128]{1,0:T(8,128)(2,1)S(1)} %collective-permute-done.7.refs_3_), channel_id=1, source_target_pairs={{0,1},{1,0},{2,3},{3,2},{4,5},{5,4},{6,7},{7,6},{8,9},{9,8},{10,11... | collective-permute-start | bytes 393224 | tf_op jit(solution)/shard_map/ppermute | solution.py:223
  19.2 12.9 %collective-permute-start.12 = (bf16[512,128]{1,0:T(8,128)(2,1)S(1)}, bf16[512,128]{1,0:T(8,128)(2,1)S(1)}, u32[]{:S(2)}, u32[]{:S(2)}) collective-permute-start(bf16[512,128]{1,0:T(8,128)(2,1)S(1)} %get-tuple-element.106), channel_id=1, source_target_pairs={{0,8},{1,9},{2,10},{3,11},{4,12},{5,13},{6,14},{7,15},{8,0},{9,1},... | collective-permute-start | bytes 393224 | tf_op jit(solution)/shard_map/ppermute | solution.py:223
  24.5 10.0 %collective-permute-start.11 = (bf16[512,128]{1,0:T(8,128)(2,1)S(1)}, bf16[512,128]{1,0:T(8,128)(2,1)S(1)}, u32[]{:S(2)}, u32[]{:S(2)}) collective-permute-start(bf16[512,128]{1,0:T(8,128)(2,1)S(1)} %get-tuple-element.102), channel_id=1, source_target_pairs={{0,8},{1,9},{2,10},{3,11},{4,12},{5,13},{6,14},{7,15},{8,0},{9,1},... | collective-permute-start | bytes 393224 | tf_op jit(solution)/shard_map/ppermute | solution.py:223

commit v3 on v2

--- a/solution.py
+++ b/solution.py
@@ -33,24 +33,24 @@
     return dot(jnp.concatenate([high, low], axis=1), ones)
 
 
-def sigmoid(x):
-    return 0.5 + 0.5 * jnp.tanh(0.5 * x)
-
-
-def layer_norm(values, mean, gain, bias):
-    centered = values - mean
+def centred(x):
+    lanes = x.shape[1]
+    eye = lax.broadcasted_iota(jnp.int32, (lanes, lanes), 0) == lax.broadcasted_iota(jnp.int32, (lanes, lanes), 1)
+    return dot(x, (jnp.where(eye, 1.0, 0.0) - 1.0 / lanes).astype(BF16))
+
+
+def normalised(centered, gain, bias):
     spread = lane_means((centered * centered).astype(BF16))
     return (centered * lax.rsqrt(spread + 1e-05) * gain + bias).astype(BF16)
 
 
-def input_norm(x, gain, bias):
-    return layer_norm(x.astype(F32), lane_means(x), gain, bias)
-
-
-def gated(normed, w):
-    half = w.shape[1] // 2
-    both = dot(normed, w)
-    return both[:, :half] * sigmoid(both[:, half:])
+def gated(normed, weights):
+    half_p = dot(normed, weights[0])
+    return half_p + half_p * jnp.tanh(dot(normed, weights[1]))
+
+
+def halved(w):
+    return (w.astype(F32) * 0.5).astype(BF16)
 
 
 def k_valid(mask_ref, first, columns, lanes):
@@ -63,54 +63,52 @@
 
 def split_weights(we_ref, wg_ref):
     half = we_ref.shape[1] // 2
-    left = jnp.concatenate([we_ref[:, :half], wg_ref[:, :half]], axis=1)
-    right = jnp.concatenate([we_ref[:, half:], wg_ref[:, half:]], axis=1)
+    left = halved(we_ref[:, :half]), halved(wg_ref[:, :half])
+    right = halved(we_ref[:, half:]), halved(wg_ref[:, half:])
     return left, right
 
 
-def right_edges(normed_ref, first, rows, w, valid):
-    right = gated(normed_ref[pl.ds(first, rows), :], w)
-    columns, lanes = valid.shape
-    return (right.reshape(rows // columns, columns, lanes) * valid).reshape(rows, lanes)
-
-
 def contract(slabs, start, out, block, columns):
-    at_once = 4
-
-    def rows_of(j):
-        return pl.ds(pl.multiple_of(j * block, block), block)
-
-    def step(g, carry):
-        js = [g * at_once + n for n in range(at_once)]
-        sums = [None if start is None else start[rows_of(j), :] for j in js]
+    at_once = min(32, block)
+    for i in range(0, block, at_once):
+        here = [pl.ds(j * block + i, at_once) for j in range(columns)]
+        sums = [None if start is None else start[rows, :] for rows in here]
         for left_ref, right_ref in slabs:
             for k in range(columns):
-                left = left_ref[pl.ds(k, block, stride=columns), :]
-                for n, j in enumerate(js):
+                left = left_ref[pl.ds(i * columns + k, at_once, stride=columns), :]
+                for j in range(columns):
                     term = left * right_ref[pl.ds(j * columns + k, 1), :]
-                    sums[n] = term if sums[n] is None else sums[n] + term
-        for n, j in enumerate(js):
-            out[rows_of(j), :] = sums[n].astype(out.dtype)
-        return carry
-
-    lax.fori_loop(0, columns // at_once, step, 0)
+                    sums[j] = term if sums[j] is None else sums[j] + term
+        for rows, value in zip(here, sums):
+            out[rows, :] = value.astype(out.dtype)
 
 
 def block_rows(me, t, rows):
     return pl.ds(pl.multiple_of(((me // SQUARE) ^ t) * rows, rows), rows)
 
 
-def edges_of(raws, lefts, rights, valids, gain, bias, weights, normed_ref, me, js, more=None):
+def right_edges(normed, weights, valids, refs):
+    right = gated(normed, weights)
+    columns, lanes = valids[0].shape
+    js = normed.shape[0] // len(refs)
+    for m, (valid, ref) in enumerate(zip(valids, refs)):
+        ref[...] = (right[m * js : (m + 1) * js, :].reshape(columns, columns, lanes) * valid).reshape(js, lanes)
+
+
+def place_rows(me, js):
+    return pl.ds(pl.multiple_of((me % SQUARE) * js, js), js)
+
+
+def edges_of(raws, lefts, rights, valids, gain, bias, weights, normed_ref, me, js):
     w_left, w_right = weights
     for m, x in enumerate(raws):
-        normed = input_norm(x, gain, bias)
-        normed_ref[m] = normed
-        lefts[m][...] = gated(normed, w_left)
-        if more is not None:
-            more(m, normed)
+        normed_ref[m] = normalised(centred(x), gain, bias)
     for m in range(len(raws)):
-        first = pl.multiple_of((me % SQUARE) * js, js)
-        rights[m][...] = right_edges(normed_ref.at[m], first, js, w_right, valids[m])
+        lefts[m][...] = gated(normed_ref[m], w_left)
+    wanted = [m for m in range(len(raws)) if rights[m] is not None]
+    if wanted:
+        normed = jnp.concatenate([normed_ref[m, place_rows(me, js), :] for m in wanted], axis=0)
+        right_edges(normed, w_right, [valids[m] for m in wanted], [rights[m] for m in wanted])
 
 
 def own_kernel(squares, block, columns, *refs):
@@ -127,15 +125,14 @@
     residues = mask_row_ref.shape[1]
     valids = [k_valid(mask_ref, (me ^ b) * columns, columns, lanes) for b in (0, CORE)]
 
-    def gates(m, normed):
-        if m < squares:
-            gates_ref[m * rows : (m + 1) * rows, :] = sigmoid(dot(normed, gate_ref[...]))
-
     edges_of(
         [slab[block_rows(me, t, rows), :] for slab in slabs for t in range(squares)],
         lefts, rights, [valids[0]] * squares + [valids[1]] * squares,
-        gain_ref[...], bias_ref[...], split_weights(we_ref, wg_ref), normed_ref, me, js, gates,
+        gain_ref[...], bias_ref[...], split_weights(we_ref, wg_ref), normed_ref, me, js,
     )
+    half_gate = halved(gate_ref[...])
+    for t in range(squares):
+        gates_ref[t * rows : (t + 1) * rows, :] = 0.5 + 0.5 * jnp.tanh(dot(normed_ref[t], half_gate))
     for t in range(squares):
         for s in range(1, squares):
             terms = [(lefts[t], rights[s]), (lefts[squares + t], rights[squares + s])]
@@ -161,24 +158,35 @@
         return out
 
     rows, js = block * columns, columns * columns
+    late = [p for p in old if p[1] == 0 and p[0] in FAR] if not new else []
+    me = take(1)[0][0]
+    raw = take(len(new) + len(late))
+    valid_ref, gain_ref, bias_ref, we_ref, wg_ref = take(5)
+    old_lefts, old_rights = take(len(old)), take(len(old) - len(late))
+    starts = [take(1)[0] if begun else None for _, _, begun in products]
+    made = [p for p in new if p[1]]
+    new_lefts, new_rights = take(len(new)), take(len(made))
+    outs = take(len(products))
+    lefts = dict(zip(old, old_lefts))
+    rights = dict(zip([p for p in old if p not in late], old_rights))
+    weights = split_weights(we_ref, wg_ref)
+    valid = lambda b: valid_ref[pl.ds(FAR.index(b) * columns, columns), :]
     if new:
-        me = take(1)[0][0]
-        raw = take(len(new))
-        valid_ref, gain_ref, bias_ref, we_ref, wg_ref = take(5)
-    old_lefts, old_rights = take(len(old)), take(len(old))
-    starts = [take(1)[0] if begun else None for _, _, begun in products]
-    new_lefts, new_rights = take(len(new)), take(len(new))
-    outs = take(len(products))
-    edges = dict(zip(old, zip(old_lefts, old_rights)))
-    if new:
+        lefts.update(zip(new, new_lefts))
+        rights.update(zip(made, new_rights))
         edges_of(
             [x[block_rows(me, t, rows) if x.shape[0] > rows else pl.ds(0, rows), :] for x, (_, t) in zip(raw, new)],
-            new_lefts, new_rights, [valid_ref[pl.ds(FAR.index(b) * columns, columns), :] for b, _ in new],
-            gain_ref[...], bias_ref[...], split_weights(we_ref, wg_ref), refs[0], me, js,
+            new_lefts, [rights.get(p) for p in new], [valid(b) for b, _ in new],
+            gain_ref[...], bias_ref[...], weights, refs[0], me, js,
         )
-        edges.update(zip(new, zip(new_lefts, new_rights)))
+    if late:
+        at = (me // SQUARE) * rows + (me % SQUARE) * js
+        x = [x[pl.ds(pl.multiple_of(at, js), js) if x.shape[0] > rows else place_rows(me, js), :] for x in raw]
+        normed = normalised(centred(jnp.concatenate(x, axis=0)), gain_ref[...], bias_ref[...])
+        rights.update({p: refs[0].at[m] for m, p in enumerate(late)})
+        right_edges(normed, weights[1], [valid(b) for b, _ in late], [rights[p] for p in late])
     for ((t, s), slabs, _), start, out in zip(products, starts, outs):
-        contract([(edges[b, t][0], edges[b, s][1]) for b in slabs], start, out, block, columns)
+        contract([(lefts[b, t], rights[b, s]) for b in slabs], start, out, block, columns)
 
 
 def last_kernel(t, n_sums, block, columns, me_ref, *refs):
@@ -192,7 +200,7 @@
         outer = outer + other[...].astype(F32)
     i_valid = i_valid_ref[t * block : (t + 1) * block, :]
     outer = outer * jnp.concatenate([i_valid * j_valid_ref[j : j + 1, :] for j in range(columns)], axis=0)
-    normed = layer_norm(outer, two_part_means(outer), norm_ref[:1, :], norm_ref[1:, :])
+    normed = normalised(outer - two_part_means(outer), norm_ref[:1, :], norm_ref[1:, :])
     projected = dot(normed, w_ref[...])
     for j in range(columns):
         turned_ref[pl.ds(j, block, stride=columns), :] = projected[j * block : (j + 1) * block, :]
@@ -226,11 +234,16 @@
     flat = pair.reshape(residues * columns, lanes)
     order = list(range(1, squares)) + [0]
     raw = {}
+    own = {t: lax.dynamic_slice_in_dim(pair, (square ^ t) * block, block, 0).reshape(rows, lanes) for t in order}
+
+    def fetch(names, after=()):
+        for b, t in names:
+            raw[b, t] = swap(lax.optimization_barrier((own[t], after))[0] if len(after) else own[t], b)
+
     whole = swap(flat, CORNER)
+    raw.update({(CORNER, t): whole for t in order})
     for t in order:
-        own = lax.dynamic_slice_in_dim(pair, (square ^ t) * block, block, 0).reshape(rows, lanes)
-        for b in (Z, Y):
-            raw[b, t] = swap(own, b)
+        fetch([(b, t) for b in (Z, Y)])
     near_whole = swap(flat, CORE)
 
     tile = lambda n, dtype=F32: ((n, lanes), dtype)
@@ -252,29 +265,28 @@
 
     def pieces(new, products):
         read = sorted({(b, u) for (t, s), slabs, *_ in products for b in slabs for u in (t, s)} - set(new))
-        operands = []
-        if new:
-            operands += [me] + [raw[p] for p in new] + [far_valid, in_gain, in_bias, w_edges, w_edge_gates]
-        operands += [lefts[p] for p in read] + [rights[p] for p in read] + [sums[ts] for ts, _, begun, _ in products if begun]
-        made = call(
+        late = [p for p in read if p not in rights]
+        made = [p for p in new if p[1]]
+        operands = [me] + [raw[p] for p in (*new, *late)] + [far_valid, in_gain, in_bias, w_edges, w_edge_gates]
+        operands += [lefts[p] for p in read] + [rights[p] for p in read if p in rights]
+        operands += [sums[ts] for ts, _, begun, _ in products if begun]
+        scratch = pltpu.VMEM((len(new), rows, lanes), BF16) if new else pltpu.VMEM((len(late), js, lanes), F32)
+        out = call(
             functools.partial(piece_kernel, tuple(new), tuple(read), tuple(p[:3] for p in products), block, columns),
             operands,
-            1 if new else 0,
-            [tile(rows)] * len(new) + [tile(js)] * len(new) + [tile(rows, dtype) for *_, dtype in products],
-            [pltpu.VMEM((len(new), rows, lanes), BF16)] if new else [],
+            1,
+            [tile(rows)] * len(new) + [tile(js)] * len(made) + [tile(rows, dtype) for *_, dtype in products],
+            [scratch],
         )
-        for n, p in enumerate(new):
-            lefts[p], rights[p] = made[n], made[len(new) + n]
-        return made[2 * len(new) :]
+        lefts.update(zip(new, out))
+        rights.update(zip(made, out[len(new) :]))
+        return out[len(new) + len(made) :]
 
     def hand_on(names, after):
-        for b, ts in names:
-            value, _ = lax.optimization_barrier((raw[b, ts[0]], after))
-            value = swap(value, CORE)
-            raw.update({(b + CORE, t): value for t in ts})
+        for b, t in names:
+            raw[b + CORE, t] = swap(lax.optimization_barrier((raw[b, t], after))[0], CORE)
 
     first, rest = order[0], order[1:]
-    raw.update({(CORNER, t): whole for t in order})
     missing = {ts: set(FAR) for ts in others}
     arrived = {}
 
@@ -293,15 +305,15 @@
                 sums[t, s] = value
             else:
                 arrived[t ^ s, s] = swap(value, SQUARE * s)
-        return lefts[step[0]]
-
-    hand_on([(Z, [first])], gates)
-    after = work([(Z, first)])
-    hand_on([(Y, [first]), (CORNER, order)], after)
-    after = work([(Y, first), (CORNER, first), (Z + CORE, first)])
+        return lefts[step[-1]]
+
+    hand_on([(Z, first), (Y, first)], gates)
+    whole_of_core = swap(lax.optimization_barrier((whole, gates))[0], CORE)
+    raw.update({(CORNER + CORE, t): whole_of_core for t in order})
+    after = work([(Z, first), (Y, first), (CORNER, first)])
     for t in rest:
-        hand_on([(Z, [t]), (Y, [t])], after)
-    work([(Y + CORE, first), (CORNER + CORE, first)])
+        hand_on([(b, t) for b in (Z, Y)], after)
+    work([(b + CORE, first) for b in (Z, Y, CORNER)])
     for t in rest:
         work([(b, t) for b in FAR])
     with jax.named_scope("own_outer"):

time: 35.8 us -> 35.1 us (0.980)
  Pallas kernels: 14.7 us -> 12.1 us
  waiting for transfers between devices: 6.72 us -> 8.75 us
    pallas_call x6 -> x5, Pallas kernels: 12.3 us -> 9.7 us  [call(): pl.pallas_call(kernel, out_shape=[jax.ShapeDtypeStruct(shape, dtype) for...]
    ppermute x13, waiting for transfers between devices: 6.72 us -> 8.75 us  [swap(): return lax.ppermute(value, 'row', [(i, i ^ bits) for i in range(size)])]
  transfers between devices with their start and end apart: 13 -> 13, of which waited for: 3 -> 5; matrix products, arithmetic and copies ran while one was open for 3% -> 3% of each run, Pallas kernels for 38% -> 31%
where the time goes in v3:
time: 35.1 us; the launch traced here: 35 us
  starting transfers between devices  12.2 us (35%)
  Pallas kernels  12.1 us (34%)
  waiting for transfers between devices  8.75 us (25%)
  local copies, waits for them, and re-layouts  1.72 us (5%)
    ppermute x13, starting transfers between devices, swap(): return lax.ppermute(value, 'row', [(i, i ^ bits) for i in range(size)])  12.2 us
    pallas_call x5, Pallas kernels, call(): pl.pallas_call(kernel, out_shape=[jax.ShapeDtypeStruct(shape, dtype) for...  9.7 us
    ppermute x13, waiting for transfers between devices, swap(): return lax.ppermute(value, 'row', [(i, i ^ bits) for i in range(size)])  8.75 us
    pallas_call x2, Pallas kernels, local(): pl.pallas_call(functools.partial(last_kernel, t, 1 + len(others), block,...  2.41 us
    reshape x1, local copies, waits for them, and re-layouts, local(): lax.dynamic_slice_in_dim(pair, (square ^ t) * block, block, 0)  1.05 us
  transfers between devices with their start and end apart: 13, of which 5 were waited for; matrix products, arithmetic and copies ran while one was open for 3% of the time, Pallas kernels for 31%

profile of v3, /device:TPU:0, one launch (start us, length us, event | category | flops | bytes accessed | tf_op | source)
XLA Modules:
  0.0 35.0 jit_solution(5441901359248367253)
XLA Ops:
  0.0 0.5 %collective-permute-start = (bf16[1024,128]{1,0:T(8,128)(2,1)}, bf16[1024,128]{1,0:T(8,128)(2,1)S(1)}, u32[]{:S(2)}, u32[]{:S(2)}) collective-permute-start(bf16[1024,128]{1,0:T(8,128)(2,1)} %bitcast.12), channel_id=1, source_target_pairs={{0,1},{1,0},{2,3},{3,2},{4,5},{5,4},{6,7},{7,6},{8,9},{9,8},{10,11... | collective-permute-start | bytes 786440 | tf_op jit(solution)/shard_map/ppermute | solution.py:231
  0.5 3.5 %collective-permute-start.4 = (bf16[1024,128]{1,0:T(8,128)(2,1)}, bf16[1024,128]{1,0:T(8,128)(2,1)S(1)}, u32[]{:S(2)}, u32[]{:S(2)}) collective-permute-start(bf16[1024,128]{1,0:T(8,128)(2,1)} %bitcast.13), channel_id=1, source_target_pairs={{0,6},{1,7},{2,4},{3,5},{4,2},{5,3},{6,0},{7,1},{8,14},{9,15},{10,... | collective-permute-start | bytes 786440 | tf_op jit(solution)/shard_map/ppermute | solution.py:231
  4.0 1.0 %dynamic-slice_bitcast_fusion = (bf16[512,128]{1,0:T(8,128)(2,1)S(1)}, bf16[512,128]{1,0:T(8,128)(2,1)S(1)}) fusion(bf16[128,8,128]{2,1,0:T(8,128)(2,1)} %param.10, s32[]{:T(128)S(6)} %select_n.13, s32[]{:T(128)S(6)} %select_n.12), kind=kLoop, calls=%fused_computation | loop fusion | bytes 524296 | tf_op jit(solution)/shard_map/reshape | solution.py:237
  5.1 0.6 %collective-permute-start.3 = (bf16[512,128]{1,0:T(8,128)(2,1)S(1)}, bf16[512,128]{1,0:T(8,128)(2,1)S(1)}, u32[]{:S(2)}, u32[]{:S(2)}) collective-permute-start(bf16[512,128]{1,0:T(8,128)(2,1)S(1)} %get-tuple-element.93), channel_id=1, source_target_pairs={{0,2},{1,3},{2,0},{3,1},{4,6},{5,7},{6,4},{7,5},{8,10},{9,11},{10,... | collective-permute-start | bytes 393224 | tf_op jit(solution)/shard_map/ppermute | solution.py:231
  5.6 0.1 collective-permute-start.2
  5.7 1.9 %collective-permute-start.6 = (bf16[512,128]{1,0:T(8,128)(2,1)S(1)}, bf16[512,128]{1,0:T(8,128)(2,1)S(1)}, u32[]{:S(2)}, u32[]{:S(2)}) collective-permute-start(bf16[512,128]{1,0:T(8,128)(2,1)S(1)} %get-tuple-element.94), channel_id=1, source_target_pairs={{0,4},{1,5},{2,6},{3,7},{4,0},{5,1},{6,2},{7,3},{8,12},{9,13},{10,... | collective-permute-start | bytes 393224 | tf_op jit(solution)/shard_map/ppermute | solution.py:231
  7.7 1.5 %collective-permute-start.1 = (bf16[512,128]{1,0:T(8,128)(2,1)S(1)}, bf16[512,128]{1,0:T(8,128)(2,1)S(1)}, u32[]{:S(2)}, u32[]{:S(2)}) collective-permute-start(bf16[512,128]{1,0:T(8,128)(2,1)S(1)} %get-tuple-element.94), channel_id=1, source_target_pairs={{0,2},{1,3},{2,0},{3,1},{4,6},{5,7},{6,4},{7,5},{8,10},{9,11},{10,... | collective-permute-start | bytes 393224 | tf_op jit(solution)/shard_map/ppermute | solution.py:231
  9.3 0.6 %copy-done.8 = f32[128]{0:T(128)S(1)} copy-done((f32[128]{0:T(128)S(1)}, f32[128]{0:T(128)}, u32[]{:S(2)}) %copy-start.8) | copy-done | bytes 536
  9.9 2.2 %own_slab.1 = (f32[1024,128]{1,0:T(8,128)S(1)}, f32[48,128]{1,0:T(8,128)S(1)}, f32[128,128]{1,0:T(8,128)S(1)}, f32[8,128]{1,0:T(8,128)S(1)}, bf16[128,128]{1,0:T...) custom-call(s32[1]{0:T(128)} %bitcast.refs_0_.me_ref, ...), custom_call_target="tpu_custom_call" | custom-call | tf_op jit(solution)/shard_map/own_slab/pallas_call | solution.py:211
  12.2 1.9 %collective-permute-done.3.refs_2_ = bf16[512,128]{1,0:T(8,128)(2,1)S(1)} collective-permute-done((bf16[512,128]{1,0:T(8,128)(2,1)S(1)}, bf16[512,128]{1,0:T(8,128)(2,1)S(1)}, u32[]{:S(2)}, u32[]{:S(2)}) %collective-permute-start.3) | collective-permute-done | bytes 131104 | tf_op jit(solution)/shard_map/ppermute | solution.py:231
  14.0 0.5 %collective-permute-done.2.refs_1_ = bf16[512,128]{1,0:T(8,128)(2,1)S(1)} collective-permute-done((bf16[512,128]{1,0:T(8,128)(2,1)S(1)}, bf16[512,128]{1,0:T(8,128)(2,1)S(1)}, u32[]{:S(2)}, u32[]{:S(2)}) %collective-permute-start.2) | collective-permute-done | bytes 131104 | tf_op jit(solution)/shard_map/ppermute | solution.py:231
  14.6 0.5 %collective-permute-start.10 = (bf16[512,128]{1,0:T(8,128)(2,1)S(1)}, bf16[512,128]{1,0:T(8,128)(2,1)S(1)}, u32[]{:S(2)}, u32[]{:S(2)}) collective-permute-start(bf16[512,128]{1,0:T(8,128)(2,1)S(1)} %collective-permute-done.3.refs_2_), channel_id=1, source_target_pairs={{0,1},{1,0},{2,3},{3,2},{4,5},{5,4},{6,7},{7,6},{8,9},{9,8},{10,11... | collective-permute-start | bytes 393224 | tf_op jit(solution)/shard_map/ppermute | solution.py:231
  15.1 1.4 %pieces.3 = (f32[512,128]{1,0:T(8,128)S(1)}, f32[512,128]{1,0:T(8,128)S(1)}, f32[512,128]{1,0:T(8,128)S(1)}, f32[64,128]{1,0:T(8,128)S(1)}, f32[64,128]{1,0:T(8,...) custom-call(s32[1]{0:T(128)} %bitcast.refs_0_.me_ref, bf16[512,128]{1,0:T(8,128)(2,1)S(1)} %collective-permute-done.2.refs_1_, ...), custom_call_target="tpu_custom_call" | custom-call | tf_op jit(solution)/shard_map/pieces/pallas_call | solution.py:211
  16.5 0.5 %collective-permute-done.6.refs_3_ = bf16[512,128]{1,0:T(8,128)(2,1)S(1)} collective-permute-done((bf16[512,128]{1,0:T(8,128)(2,1)S(1)}, bf16[512,128]{1,0:T(8,128)(2,1)S(1)}, u32[]{:S(2)}, u32[]{:S(2)}) %collective-permute-start.6) | collective-permute-done | bytes 131104 | tf_op jit(solution)/shard_map/ppermute | solution.py:231
  17.0 0.5 %collective-permute-start.7 = (bf16[512,128]{1,0:T(8,128)(2,1)S(1)}, bf16[512,128]{1,0:T(8,128)(2,1)S(1)}, u32[]{:S(2)}, u32[]{:S(2)}) collective-permute-start(bf16[512,128]{1,0:T(8,128)(2,1)S(1)} %collective-permute-done.6.refs_3_), channel_id=1, source_target_pairs={{0,1},{1,0},{2,3},{3,2},{4,5},{5,4},{6,7},{7,6},{8,9},{9,8},{10,11... | collective-permute-start | bytes 393224 | tf_op jit(solution)/shard_map/ppermute | solution.py:231
  17.5 1.4 %pieces.4 = (f32[512,128]{1,0:T(8,128)S(1)}, f32[512,128]{1,0:T(8,128)S(1)}, f32[512,128]{1,0:T(8,128)S(1)}, f32[64,128]{1,0:T(8,128)S(1)}, f32[64,128]{1,0:T(8,...) custom-call(s32[1]{0:T(128)} %bitcast.refs_0_.me_ref, ...), custom_call_target="tpu_custom_call" | custom-call | tf_op jit(solution)/shard_map/pieces/pallas_call | solution.py:211
  19.0 2.7 %collective-permute-start.12 = (bf16[512,128]{1,0:T(8,128)(2,1)S(1)}, bf16[512,128]{1,0:T(8,128)(2,1)S(1)}, u32[]{:S(2)}, u32[]{:S(2)}) collective-permute-start(bf16[512,128]{1,0:T(8,128)(2,1)S(1)} %get-tuple-element.92), channel_id=1, source_target_pairs={{0,8},{1,9},{2,10},{3,11},{4,12},{5,13},{6,14},{7,15},{8,0},{9,1},... | collective-permute-start | bytes 393224 | tf_op jit(solution)/shard_map/ppermute | solution.py:231
  21.6 2.0 %pieces.5 = (f32[512,128]{1,0:T(8,128)S(1)}, f32[512,128]{1,0:T(8,128)S(1)}, f32[512,128]{1,0:T(8,128)S(1)}, f32[512,128]{1,0:T(8,128)S(1)}, f32[512,128]{1,0:T(...) custom-call(s32[1]{0:T(128)} %bitcast.refs_0_.me_ref, ...), custom_call_target="tpu_custom_call" | custom-call | tf_op jit(solution)/shard_map/pieces/pallas_call | solution.py:211
  23.7 0.4 %collective-permute-start.11 = (bf16[512,128]{1,0:T(8,128)(2,1)S(1)}, bf16[512,128]{1,0:T(8,128)(2,1)S(1)}, u32[]{:S(2)}, u32[]{:S(2)}) collective-permute-start(bf16[512,128]{1,0:T(8,128)(2,1)S(1)} %get-tuple-element.88), channel_id=1, source_target_pairs={{0,8},{1,9},{2,10},{3,11},{4,12},{5,13},{6,14},{7,15},{8,0},{9,1},... | collective-permute-start | bytes 393224 | tf_op jit(solution)/shard_map/ppermute | solution.py:231
  24.1 2.7 %own_outer.1 = (f32[512,128]{1,0:T(8,128)S(1)}, f32[512,128]{1,0:T(8,128)S(1)}) custom-call(s32[1]{0:T(128)} %bitcast.refs_0_.me_ref, bf16[512,128]{1,0:T(8,128)(2,1)S(1)} %collective-permute-done.1.refs_1_, bf16[512,128]{1,0:T(8,128)(2,1)S(1)} %collective-permute-done.5.refs_2_, bf16[512,128]{1,0:T(8,128)(2,1)S(1)} %collective-permute-done.6.refs_3_, ...), custom_call_target="tpu_custom_call" | custom-call | tf_op jit(solution)/shard_map/own_outer/pallas_call | solution.py:211
  26.7 5.2 %collective-permute-done.12.refs_3_ = bf16[512,128]{1,0:T(8,128)(2,1)S(1)} collective-permute-done((bf16[512,128]{1,0:T(8,128)(2,1)S(1)}, bf16[512,128]{1,0:T(8,128)(2,1)S(1)}, u32[]{:S(2)}, u32[]{:S(2)}) %collective-permute-start.12) | collective-permute-done | bytes 131104 | tf_op jit(solution)/shard_map/ppermute | solution.py:231
  31.9 1.2 %update.2.refs_7_ = bf16[1024,128]{1,0:T(8,128)(2,1)} custom-call(s32[1]{0:T(128)} %bitcast.refs_0_.me_ref, f32[128,128]{1,0:T(8,128)S(1)} %get-tuple-element.49.refs_0_, f32[8,128]{1,0:T(8,128)S(1)} %get-tuple-element.50.refs_1_, f32[512,128]{1,0:T(8,128)S(1)} %get-tuple-element.91.refs_2_, bf16[512,128]{1,0:T(8,128)(2,1)S(1)} %collective-permute-done.12.refs_3_, ...), custom_call_target="tpu_custom_call" | custom-call | tf_op jit(solution)/shard_map/update/pallas_call | solution.py:328
  33.1 0.7 %collective-permute-done.11.refs_3_ = bf16[512,128]{1,0:T(8,128)(2,1)S(1)} collective-permute-done((bf16[512,128]{1,0:T(8,128)(2,1)S(1)}, bf16[512,128]{1,0:T(8,128)(2,1)S(1)}, u32[]{:S(2)}, u32[]{:S(2)}) %collective-permute-start.11) | collective-permute-done | bytes 131104 | tf_op jit(solution)/shard_map/ppermute | solution.py:231
  33.8 1.2 %update.3 = bf16[1024,128]{1,0:T(8,128)(2,1)} custom-call(s32[1]{0:T(128)} %bitcast.refs_0_.me_ref, f32[128,128]{1,0:T(8,128)S(1)} %get-tuple-element.49.refs_0_, f32[8,128]{1,0:T(8,128)S(1)} %get-tuple-element.50.refs_1_, f32[512,128]{1,0:T(8,128)S(1)} %get-tuple-element.87.refs_2_, ...), custom_call_target="tpu_custom_call", output_to_operand_aliasing={{}: (8, {})} | custom-call | tf_op jit(solution)/shard_map/update/pallas_call | solution.py:328
  (30 shorter events, 0.2 us)
Async XLA Ops:
  0.0 7.7 %collective-permute-start = (bf16[1024,128]{1,0:T(8,128)(2,1)}, bf16[1024,128]{1,0:T(8,128)(2,1)S(1)}, u32[]{:S(2)}, u32[]{:S(2)}) collective-permute-start(bf16[1024,128]{1,0:T(8,128)(2,1)} %bitcast.12), channel_id=1, source_target_pairs={{0,1},{1,0},{2,3},{3,2},{4,5},{5,4},{6,7},{7,6},{8,9},{9,8},{10,11... | collective-permute-start | bytes 786440 | tf_op jit(solution)/shard_map/ppermute | solution.py:231
  0.5 11.6 %collective-permute-start.4 = (bf16[1024,128]{1,0:T(8,128)(2,1)}, bf16[1024,128]{1,0:T(8,128)(2,1)S(1)}, u32[]{:S(2)}, u32[]{:S(2)}) collective-permute-start(bf16[1024,128]{1,0:T(8,128)(2,1)} %bitcast.13), channel_id=1, source_target_pairs={{0,6},{1,7},{2,4},{3,5},{4,2},{5,3},{6,0},{7,1},{8,14},{9,15},{10,... | collective-permute-start | bytes 786440 | tf_op jit(solution)/shard_map/ppermute | solution.py:231
  4.0 5.2 %copy-start = (bf16[128,256]{1,0:T(8,128)(2,1)S(1)}, bf16[128,256]{1,0:T(8,128)(2,1)}, u32[]{:S(2)}) copy-start(bf16[128,256]{1,0:T(8,128)(2,1)} %refs_10_.5) | copy-start | bytes 196612
  4.0 5.2 %copy-start.1 = (bf16[128,256]{1,0:T(8,128)(2,1)S(1)}, bf16[128,256]{1,0:T(8,128)(2,1)}, u32[]{:S(2)}) copy-start(bf16[128,256]{1,0:T(8,128)(2,1)} %refs_11_.3) | copy-start | bytes 196612
  4.0 5.2 %copy-start.2 = (bf16[128,8,128]{2,1,0:T(8,128)(2,1)S(1)}, bf16[128,8,128]{2,1,0:T(8,128)(2,1)}, u32[]{:S(2)}) copy-start(bf16[128,8,128]{2,1,0:T(8,128)(2,1)} %param.10) | copy-start | bytes 786436
  4.0 5.2 %copy-start.3 = (bf16[128,128]{1,0:T(8,128)(2,1)S(1)}, bf16[128,128]{1,0:T(8,128)(2,1)}, u32[]{:S(2)}) copy-start(bf16[128,128]{1,0:T(8,128)(2,1)} %refs_9_.1) | copy-start | bytes 98308
  4.0 5.2 %copy-start.4 = (bf16[128,128]{1,0:T(8,128)(2,1)S(1)}, bf16[128,128]{1,0:T(8,128)(2,1)}, u32[]{:S(2)}) copy-start(bf16[128,128]{1,0:T(8,128)(2,1)} %refs_10_.3) | copy-start | bytes 98308
  5.1 9.0 %collective-permute-start.3 = (bf16[512,128]{1,0:T(8,128)(2,1)S(1)}, bf16[512,128]{1,0:T(8,128)(2,1)S(1)}, u32[]{:S(2)}, u32[]{:S(2)}) collective-permute-start(bf16[512,128]{1,0:T(8,128)(2,1)S(1)} %get-tuple-element.93), channel_id=1, source_target_pairs={{0,2},{1,3},{2,0},{3,1},{4,6},{5,7},{6,4},{7,5},{8,10},{9,11},{10,... | collective-permute-start | bytes 393224 | tf_op jit(solution)/shard_map/ppermute | solution.py:231
  5.6 8.9 %collective-permute-start.2 = (bf16[512,128]{1,0:T(8,128)(2,1)S(1)}, bf16[512,128]{1,0:T(8,128)(2,1)S(1)}, u32[]{:S(2)}, u32[]{:S(2)}) collective-permute-start(bf16[512,128]{1,0:T(8,128)(2,1)S(1)} %get-tuple-element.93), channel_id=1, source_target_pairs={{0,4},{1,5},{2,6},{3,7},{4,0},{5,1},{6,2},{7,3},{8,12},{9,13},{10,... | collective-permute-start | bytes 393224 | tf_op jit(solution)/shard_map/ppermute | solution.py:231
  5.7 11.3 %collective-permute-start.6 = (bf16[512,128]{1,0:T(8,128)(2,1)S(1)}, bf16[512,128]{1,0:T(8,128)(2,1)S(1)}, u32[]{:S(2)}, u32[]{:S(2)}) collective-permute-start(bf16[512,128]{1,0:T(8,128)(2,1)S(1)} %get-tuple-element.94), channel_id=1, source_target_pairs={{0,4},{1,5},{2,6},{3,7},{4,0},{5,1},{6,2},{7,3},{8,12},{9,13},{10,... | collective-permute-start | bytes 393224 | tf_op jit(solution)/shard_map/ppermute | solution.py:231
  7.7 9.3 %collective-permute-start.1 = (bf16[512,128]{1,0:T(8,128)(2,1)S(1)}, bf16[512,128]{1,0:T(8,128)(2,1)S(1)}, u32[]{:S(2)}, u32[]{:S(2)}) collective-permute-start(bf16[512,128]{1,0:T(8,128)(2,1)S(1)} %get-tuple-element.94), channel_id=1, source_target_pairs={{0,2},{1,3},{2,0},{3,1},{4,6},{5,7},{6,4},{7,5},{8,10},{9,11},{10,... | collective-permute-start | bytes 393224 | tf_op jit(solution)/shard_map/ppermute | solution.py:231
  9.2 0.7 %copy-start.8 = (f32[128]{0:T(128)S(1)}, f32[128]{0:T(128)}, u32[]{:S(2)}) copy-start(f32[128]{0:T(128)} %param.16) | copy-start | bytes 1540
  9.2 0.7 %copy-start.9 = (f32[128]{0:T(128)S(1)}, f32[128]{0:T(128)}, u32[]{:S(2)}) copy-start(f32[128]{0:T(128)} %param.17) | copy-start | bytes 1540
  9.2 0.7 %copy-start.5 = (f32[128]{0:T(128)S(1)}, f32[128]{0:T(128)}, u32[]{:S(2)}) copy-start(f32[128]{0:T(128)} %param.12) | copy-start | bytes 1540
  9.2 0.7 %copy-start.6 = (f32[128]{0:T(128)S(1)}, f32[128]{0:T(128)}, u32[]{:S(2)}) copy-start(f32[128]{0:T(128)} %param.13) | copy-start | bytes 1540
  9.2 0.7 %copy-start.7 = (s32[128]{0:T(128)S(1)}, s32[128]{0:T(128)}, u32[]{:S(2)}) copy-start(s32[128]{0:T(128)} %refs_1_.1) | copy-start | bytes 1540
  12.1 5.4 %collective-permute-start.8 = (bf16[1024,128]{1,0:T(8,128)(2,1)S(1)}, bf16[1024,128]{1,0:T(8,128)(2,1)S(1)}, u32[]{:S(2)}, u32[]{:S(2)}) collective-permute-start(bf16[1024,128]{1,0:T(8,128)(2,1)S(1)} %collective-permute-done.4.refs_3_.refs_5_), channel_id=1, source_target_pairs={{0,1},{1,0},{2,3},{3,2},{4,5},{5,4},{6,7},{7,6},{8,9},{9,8},{10,11... | collective-permute-start | bytes 786440 | tf_op jit(solution)/shard_map/ppermute | solution.py:231
  14.6 2.9 %collective-permute-start.9 = (bf16[512,128]{1,0:T(8,128)(2,1)S(1)}, bf16[512,128]{1,0:T(8,128)(2,1)S(1)}, u32[]{:S(2)}, u32[]{:S(2)}) collective-permute-start(bf16[512,128]{1,0:T(8,128)(2,1)S(1)} %collective-permute-done.2.refs_1_), channel_id=1, source_target_pairs={{0,1},{1,0},{2,3},{3,2},{4,5},{5,4},{6,7},{7,6},{8,9},{9,8},{10,11... | collective-permute-start | bytes 393224 | tf_op jit(solution)/shard_map/ppermute | solution.py:231
  14.6 2.9 %collective-permute-start.10 = (bf16[512,128]{1,0:T(8,128)(2,1)S(1)}, bf16[512,128]{1,0:T(8,128)(2,1)S(1)}, u32[]{:S(2)}, u32[]{:S(2)}) collective-permute-start(bf16[512,128]{1,0:T(8,128)(2,1)S(1)} %collective-permute-done.3.refs_2_), channel_id=1, source_target_pairs={{0,1},{1,0},{2,3},{3,2},{4,5},{5,4},{6,7},{7,6},{8,9},{9,8},{10,11... | collective-permute-start | bytes 393224 | tf_op jit(solution)/shard_map/ppermute | solution.py:231
  17.0 4.6 %collective-permute-start.5 = (bf16[512,128]{1,0:T(8,128)(2,1)S(1)}, bf16[512,128]{1,0:T(8,128)(2,1)S(1)}, u32[]{:S(2)}, u32[]{:S(2)}) collective-permute-start(bf16[512,128]{1,0:T(8,128)(2,1)S(1)} %collective-permute-done.1.refs_1_), channel_id=1, source_target_pairs={{0,1},{1,0},{2,3},{3,2},{4,5},{5,4},{6,7},{7,6},{8,9},{9,8},{10,11... | collective-permute-start | bytes 393224 | tf_op jit(solution)/shard_map/ppermute | solution.py:231
  17.0 4.6 %collective-permute-start.7 = (bf16[512,128]{1,0:T(8,128)(2,1)S(1)}, bf16[512,128]{1,0:T(8,128)(2,1)S(1)}, u32[]{:S(2)}, u32[]{:S(2)}) collective-permute-start(bf16[512,128]{1,0:T(8,128)(2,1)S(1)} %collective-permute-done.6.refs_3_), channel_id=1, source_target_pairs={{0,1},{1,0},{2,3},{3,2},{4,5},{5,4},{6,7},{7,6},{8,9},{9,8},{10,11... | collective-permute-start | bytes 393224 | tf_op jit(solution)/shard_map/ppermute | solution.py:231
  19.0 12.9 %collective-permute-start.12 = (bf16[512,128]{1,0:T(8,128)(2,1)S(1)}, bf16[512,128]{1,0:T(8,128)(2,1)S(1)}, u32[]{:S(2)}, u32[]{:S(2)}) collective-permute-start(bf16[512,128]{1,0:T(8,128)(2,1)S(1)} %get-tuple-element.92), channel_id=1, source_target_pairs={{0,8},{1,9},{2,10},{3,11},{4,12},{5,13},{6,14},{7,15},{8,0},{9,1},... | collective-permute-start | bytes 393224 | tf_op jit(solution)/shard_map/ppermute | solution.py:231
  23.7 10.1 %collective-permute-start.11 = (bf16[512,128]{1,0:T(8,128)(2,1)S(1)}, bf16[512,128]{1,0:T(8,128)(2,1)S(1)}, u32[]{:S(2)}, u32[]{:S(2)}) collective-permute-start(bf16[512,128]{1,0:T(8,128)(2,1)S(1)} %get-tuple-element.88), channel_id=1, source_target_pairs={{0,8},{1,9},{2,10},{3,11},{4,12},{5,13},{6,14},{7,15},{8,0},{9,1},... | collective-permute-start | bytes 393224 | tf_op jit(solution)/shard_map/ppermute | solution.py:231

commit v4 on v3

--- a/solution.py
+++ b/solution.py
@@ -187,6 +187,8 @@
         right_edges(normed, weights[1], [valid(b) for b, _ in late], [rights[p] for p in late])
     for ((t, s), slabs, _), start, out in zip(products, starts, outs):
         contract([(lefts[b, t], rights[b, s]) for b in slabs], start, out, block, columns)
+        if s == 0:
+            out[...] = out[...] - two_part_means(out[...])
 
 
 def last_kernel(t, n_sums, block, columns, me_ref, *refs):
@@ -197,10 +199,10 @@
     rows = block * columns
     outer = sums[0][...]
     for other in sums[1:]:
-        outer = outer + other[...].astype(F32)
+        outer = outer + centred(other[...])
     i_valid = i_valid_ref[t * block : (t + 1) * block, :]
     outer = outer * jnp.concatenate([i_valid * j_valid_ref[j : j + 1, :] for j in range(columns)], axis=0)
-    normed = normalised(outer - two_part_means(outer), norm_ref[:1, :], norm_ref[1:, :])
+    normed = normalised(outer, norm_ref[:1, :], norm_ref[1:, :])
     projected = dot(normed, w_ref[...])
     for j in range(columns):
         turned_ref[pl.ds(j, block, stride=columns), :] = projected[j * block : (j + 1) * block, :]

time: 35.1 us -> 35.1 us (level)
  waiting for transfers between devices: 8.75 us -> 7.87 us
  Pallas kernels: 12.1 us -> 12.9 us
    pallas_call x5, Pallas kernels: 9.7 us -> 10.6 us  [call(): pl.pallas_call(kernel, out_shape=[jax.ShapeDtypeStruct(shape, dtype) for...]
    ppermute x13, waiting for transfers between devices: 8.75 us -> 7.87 us  [swap(): return lax.ppermute(value, 'row', [(i, i ^ bits) for i in range(size)])]
  transfers between devices with their start and end apart: 13 -> 13, of which waited for: 5 -> 5; matrix products, arithmetic and copies ran while one was open for 3% -> 3% of each run, Pallas kernels for 31% -> 34%
where the time goes in v4:
time: 35.1 us; the launch traced here: 34.9 us
  Pallas kernels  12.9 us (37%)
  starting transfers between devices  12.2 us (35%)
  waiting for transfers between devices  7.87 us (22%)
  local copies, waits for them, and re-layouts  1.72 us (5%)
    ppermute x13, starting transfers between devices, swap(): return lax.ppermute(value, 'row', [(i, i ^ bits) for i in range(size)])  12.2 us
    pallas_call x5, Pallas kernels, call(): pl.pallas_call(kernel, out_shape=[jax.ShapeDtypeStruct(shape, dtype) for...  10.6 us
    ppermute x13, waiting for transfers between devices, swap(): return lax.ppermute(value, 'row', [(i, i ^ bits) for i in range(size)])  7.87 us
    pallas_call x2, Pallas kernels, local(): pl.pallas_call(functools.partial(last_kernel, t, 1 + len(others), block,...  2.29 us
    reshape x1, local copies, waits for them, and re-layouts, local(): lax.dynamic_slice_in_dim(pair, (square ^ t) * block, block, 0)  1.05 us
  transfers between devices with their start and end apart: 13, of which 5 were waited for; matrix products, arithmetic and copies ran while one was open for 3% of the time, Pallas kernels for 34%

profile of v4, /device:TPU:0, one launch (start us, length us, event | category | flops | bytes accessed | tf_op | source)
XLA Modules:
  0.0 34.9 jit_solution(18378844729928721753)
XLA Ops:
  0.0 0.5 %collective-permute-start = (bf16[1024,128]{1,0:T(8,128)(2,1)}, bf16[1024,128]{1,0:T(8,128)(2,1)S(1)}, u32[]{:S(2)}, u32[]{:S(2)}) collective-permute-start(bf16[1024,128]{1,0:T(8,128)(2,1)} %bitcast.12), channel_id=1, source_target_pairs={{0,1},{1,0},{2,3},{3,2},{4,5},{5,4},{6,7},{7,6},{8,9},{9,8},{10,11... | collective-permute-start | bytes 786440 | tf_op jit(solution)/shard_map/ppermute | solution.py:233
  0.5 3.5 %collective-permute-start.4 = (bf16[1024,128]{1,0:T(8,128)(2,1)}, bf16[1024,128]{1,0:T(8,128)(2,1)S(1)}, u32[]{:S(2)}, u32[]{:S(2)}) collective-permute-start(bf16[1024,128]{1,0:T(8,128)(2,1)} %bitcast.13), channel_id=1, source_target_pairs={{0,6},{1,7},{2,4},{3,5},{4,2},{5,3},{6,0},{7,1},{8,14},{9,15},{10,... | collective-permute-start | bytes 786440 | tf_op jit(solution)/shard_map/ppermute | solution.py:233
  4.0 1.0 %dynamic-slice_bitcast_fusion = (bf16[512,128]{1,0:T(8,128)(2,1)S(1)}, bf16[512,128]{1,0:T(8,128)(2,1)S(1)}) fusion(bf16[128,8,128]{2,1,0:T(8,128)(2,1)} %param.10, s32[]{:T(128)S(6)} %select_n.13, s32[]{:T(128)S(6)} %select_n.12), kind=kLoop, calls=%fused_computation | loop fusion | bytes 524296 | tf_op jit(solution)/shard_map/reshape | solution.py:239
  5.1 0.6 %collective-permute-start.3 = (bf16[512,128]{1,0:T(8,128)(2,1)S(1)}, bf16[512,128]{1,0:T(8,128)(2,1)S(1)}, u32[]{:S(2)}, u32[]{:S(2)}) collective-permute-start(bf16[512,128]{1,0:T(8,128)(2,1)S(1)} %get-tuple-element.93), channel_id=1, source_target_pairs={{0,2},{1,3},{2,0},{3,1},{4,6},{5,7},{6,4},{7,5},{8,10},{9,11},{10,... | collective-permute-start | bytes 393224 | tf_op jit(solution)/shard_map/ppermute | solution.py:233
  5.6 0.1 collective-permute-start.2
  5.7 1.9 %collective-permute-start.6 = (bf16[512,128]{1,0:T(8,128)(2,1)S(1)}, bf16[512,128]{1,0:T(8,128)(2,1)S(1)}, u32[]{:S(2)}, u32[]{:S(2)}) collective-permute-start(bf16[512,128]{1,0:T(8,128)(2,1)S(1)} %get-tuple-element.94), channel_id=1, source_target_pairs={{0,4},{1,5},{2,6},{3,7},{4,0},{5,1},{6,2},{7,3},{8,12},{9,13},{10,... | collective-permute-start | bytes 393224 | tf_op jit(solution)/shard_map/ppermute | solution.py:233
  7.7 1.5 %collective-permute-start.1 = (bf16[512,128]{1,0:T(8,128)(2,1)S(1)}, bf16[512,128]{1,0:T(8,128)(2,1)S(1)}, u32[]{:S(2)}, u32[]{:S(2)}) collective-permute-start(bf16[512,128]{1,0:T(8,128)(2,1)S(1)} %get-tuple-element.94), channel_id=1, source_target_pairs={{0,2},{1,3},{2,0},{3,1},{4,6},{5,7},{6,4},{7,5},{8,10},{9,11},{10,... | collective-permute-start | bytes 393224 | tf_op jit(solution)/shard_map/ppermute | solution.py:233
  9.3 0.6 %copy-done.8 = f32[128]{0:T(128)S(1)} copy-done((f32[128]{0:T(128)S(1)}, f32[128]{0:T(128)}, u32[]{:S(2)}) %copy-start.8) | copy-done | bytes 536
  9.9 2.2 %own_slab.1 = (f32[1024,128]{1,0:T(8,128)S(1)}, f32[48,128]{1,0:T(8,128)S(1)}, f32[128,128]{1,0:T(8,128)S(1)}, f32[8,128]{1,0:T(8,128)S(1)}, bf16[128,128]{1,0:T...) custom-call(s32[1]{0:T(128)} %bitcast.refs_0_.me_ref, ...), custom_call_target="tpu_custom_call" | custom-call | tf_op jit(solution)/shard_map/own_slab/pallas_call | solution.py:213
  12.2 1.9 %collective-permute-done.3.refs_2_ = bf16[512,128]{1,0:T(8,128)(2,1)S(1)} collective-permute-done((bf16[512,128]{1,0:T(8,128)(2,1)S(1)}, bf16[512,128]{1,0:T(8,128)(2,1)S(1)}, u32[]{:S(2)}, u32[]{:S(2)}) %collective-permute-start.3) | collective-permute-done | bytes 131104 | tf_op jit(solution)/shard_map/ppermute | solution.py:233
  14.0 0.5 %collective-permute-done.2.refs_1_ = bf16[512,128]{1,0:T(8,128)(2,1)S(1)} collective-permute-done((bf16[512,128]{1,0:T(8,128)(2,1)S(1)}, bf16[512,128]{1,0:T(8,128)(2,1)S(1)}, u32[]{:S(2)}, u32[]{:S(2)}) %collective-permute-start.2) | collective-permute-done | bytes 131104 | tf_op jit(solution)/shard_map/ppermute | solution.py:233
  14.6 0.5 %collective-permute-start.10 = (bf16[512,128]{1,0:T(8,128)(2,1)S(1)}, bf16[512,128]{1,0:T(8,128)(2,1)S(1)}, u32[]{:S(2)}, u32[]{:S(2)}) collective-permute-start(bf16[512,128]{1,0:T(8,128)(2,1)S(1)} %collective-permute-done.3.refs_2_), channel_id=1, source_target_pairs={{0,1},{1,0},{2,3},{3,2},{4,5},{5,4},{6,7},{7,6},{8,9},{9,8},{10,11... | collective-permute-start | bytes 393224 | tf_op jit(solution)/shard_map/ppermute | solution.py:233
  15.1 1.4 %pieces.3 = (f32[512,128]{1,0:T(8,128)S(1)}, f32[512,128]{1,0:T(8,128)S(1)}, f32[512,128]{1,0:T(8,128)S(1)}, f32[64,128]{1,0:T(8,128)S(1)}, f32[64,128]{1,0:T(8,...) custom-call(s32[1]{0:T(128)} %bitcast.refs_0_.me_ref, bf16[512,128]{1,0:T(8,128)(2,1)S(1)} %collective-permute-done.2.refs_1_, ...), custom_call_target="tpu_custom_call" | custom-call | tf_op jit(solution)/shard_map/pieces/pallas_call | solution.py:213
  16.5 0.5 %collective-permute-done.6.refs_3_ = bf16[512,128]{1,0:T(8,128)(2,1)S(1)} collective-permute-done((bf16[512,128]{1,0:T(8,128)(2,1)S(1)}, bf16[512,128]{1,0:T(8,128)(2,1)S(1)}, u32[]{:S(2)}, u32[]{:S(2)}) %collective-permute-start.6) | collective-permute-done | bytes 131104 | tf_op jit(solution)/shard_map/ppermute | solution.py:233
  17.0 0.5 %collective-permute-start.7 = (bf16[512,128]{1,0:T(8,128)(2,1)S(1)}, bf16[512,128]{1,0:T(8,128)(2,1)S(1)}, u32[]{:S(2)}, u32[]{:S(2)}) collective-permute-start(bf16[512,128]{1,0:T(8,128)(2,1)S(1)} %collective-permute-done.6.refs_3_), channel_id=1, source_target_pairs={{0,1},{1,0},{2,3},{3,2},{4,5},{5,4},{6,7},{7,6},{8,9},{9,8},{10,11... | collective-permute-start | bytes 393224 | tf_op jit(solution)/shard_map/ppermute | solution.py:233
  17.5 1.4 %pieces.4 = (f32[512,128]{1,0:T(8,128)S(1)}, f32[512,128]{1,0:T(8,128)S(1)}, f32[512,128]{1,0:T(8,128)S(1)}, f32[64,128]{1,0:T(8,128)S(1)}, f32[64,128]{1,0:T(8,...) custom-call(s32[1]{0:T(128)} %bitcast.refs_0_.me_ref, ...), custom_call_target="tpu_custom_call" | custom-call | tf_op jit(solution)/shard_map/pieces/pallas_call | solution.py:213
  19.0 2.7 %collective-permute-start.12 = (bf16[512,128]{1,0:T(8,128)(2,1)S(1)}, bf16[512,128]{1,0:T(8,128)(2,1)S(1)}, u32[]{:S(2)}, u32[]{:S(2)}) collective-permute-start(bf16[512,128]{1,0:T(8,128)(2,1)S(1)} %get-tuple-element.92), channel_id=1, source_target_pairs={{0,8},{1,9},{2,10},{3,11},{4,12},{5,13},{6,14},{7,15},{8,0},{9,1},... | collective-permute-start | bytes 393224 | tf_op jit(solution)/shard_map/ppermute | solution.py:233
  21.6 2.0 %pieces.5 = (f32[512,128]{1,0:T(8,128)S(1)}, f32[512,128]{1,0:T(8,128)S(1)}, f32[512,128]{1,0:T(8,128)S(1)}, f32[512,128]{1,0:T(8,128)S(1)}, f32[512,128]{1,0:T(...) custom-call(s32[1]{0:T(128)} %bitcast.refs_0_.me_ref, ...), custom_call_target="tpu_custom_call" | custom-call | tf_op jit(solution)/shard_map/pieces/pallas_call | solution.py:213
  23.7 0.4 %collective-permute-start.11 = (bf16[512,128]{1,0:T(8,128)(2,1)S(1)}, bf16[512,128]{1,0:T(8,128)(2,1)S(1)}, u32[]{:S(2)}, u32[]{:S(2)}) collective-permute-start(bf16[512,128]{1,0:T(8,128)(2,1)S(1)} %get-tuple-element.88), channel_id=1, source_target_pairs={{0,8},{1,9},{2,10},{3,11},{4,12},{5,13},{6,14},{7,15},{8,0},{9,1},... | collective-permute-start | bytes 393224 | tf_op jit(solution)/shard_map/ppermute | solution.py:233
  24.1 3.6 %own_outer.1 = (f32[512,128]{1,0:T(8,128)S(1)}, f32[512,128]{1,0:T(8,128)S(1)}) custom-call(s32[1]{0:T(128)} %bitcast.refs_0_.me_ref, bf16[512,128]{1,0:T(8,128)(2,1)S(1)} %collective-permute-done.1.refs_1_, bf16[512,128]{1,0:T(8,128)(2,1)S(1)} %collective-permute-done.5.refs_2_, bf16[512,128]{1,0:T(8,128)(2,1)S(1)} %collective-permute-done.6.refs_3_, ...), custom_call_target="tpu_custom_call" | custom-call | tf_op jit(solution)/shard_map/own_outer/pallas_call | solution.py:213
  27.7 4.2 %collective-permute-done.12.refs_3_ = bf16[512,128]{1,0:T(8,128)(2,1)S(1)} collective-permute-done((bf16[512,128]{1,0:T(8,128)(2,1)S(1)}, bf16[512,128]{1,0:T(8,128)(2,1)S(1)}, u32[]{:S(2)}, u32[]{:S(2)}) %collective-permute-start.12) | collective-permute-done | bytes 131104 | tf_op jit(solution)/shard_map/ppermute | solution.py:233
  31.9 1.1 %update.2.refs_7_ = bf16[1024,128]{1,0:T(8,128)(2,1)} custom-call(s32[1]{0:T(128)} %bitcast.refs_0_.me_ref, f32[128,128]{1,0:T(8,128)S(1)} %get-tuple-element.49.refs_0_, f32[8,128]{1,0:T(8,128)S(1)} %get-tuple-element.50.refs_1_, f32[512,128]{1,0:T(8,128)S(1)} %get-tuple-element.91.refs_2_, bf16[512,128]{1,0:T(8,128)(2,1)S(1)} %collective-permute-done.12.refs_3_, ...), custom_call_target="tpu_custom_call" | custom-call | tf_op jit(solution)/shard_map/update/pallas_call | solution.py:330
  33.0 0.7 %collective-permute-done.11.refs_3_ = bf16[512,128]{1,0:T(8,128)(2,1)S(1)} collective-permute-done((bf16[512,128]{1,0:T(8,128)(2,1)S(1)}, bf16[512,128]{1,0:T(8,128)(2,1)S(1)}, u32[]{:S(2)}, u32[]{:S(2)}) %collective-permute-start.11) | collective-permute-done | bytes 131104 | tf_op jit(solution)/shard_map/ppermute | solution.py:233
  33.8 1.1 %update.3 = bf16[1024,128]{1,0:T(8,128)(2,1)} custom-call(s32[1]{0:T(128)} %bitcast.refs_0_.me_ref, f32[128,128]{1,0:T(8,128)S(1)} %get-tuple-element.49.refs_0_, f32[8,128]{1,0:T(8,128)S(1)} %get-tuple-element.50.refs_1_, f32[512,128]{1,0:T(8,128)S(1)} %get-tuple-element.87.refs_2_, ...), custom_call_target="tpu_custom_call", output_to_operand_aliasing={{}: (8, {})} | custom-call | tf_op jit(solution)/shard_map/update/pallas_call | solution.py:330
  (30 shorter events, 0.2 us)
Async XLA Ops:
  0.0 7.7 %collective-permute-start = (bf16[1024,128]{1,0:T(8,128)(2,1)}, bf16[1024,128]{1,0:T(8,128)(2,1)S(1)}, u32[]{:S(2)}, u32[]{:S(2)}) collective-permute-start(bf16[1024,128]{1,0:T(8,128)(2,1)} %bitcast.12), channel_id=1, source_target_pairs={{0,1},{1,0},{2,3},{3,2},{4,5},{5,4},{6,7},{7,6},{8,9},{9,8},{10,11... | collective-permute-start | bytes 786440 | tf_op jit(solution)/shard_map/ppermute | solution.py:233
  0.5 11.6 %collective-permute-start.4 = (bf16[1024,128]{1,0:T(8,128)(2,1)}, bf16[1024,128]{1,0:T(8,128)(2,1)S(1)}, u32[]{:S(2)}, u32[]{:S(2)}) collective-permute-start(bf16[1024,128]{1,0:T(8,128)(2,1)} %bitcast.13), channel_id=1, source_target_pairs={{0,6},{1,7},{2,4},{3,5},{4,2},{5,3},{6,0},{7,1},{8,14},{9,15},{10,... | collective-permute-start | bytes 786440 | tf_op jit(solution)/shard_map/ppermute | solution.py:233
  4.0 5.2 %copy-start = (bf16[128,256]{1,0:T(8,128)(2,1)S(1)}, bf16[128,256]{1,0:T(8,128)(2,1)}, u32[]{:S(2)}) copy-start(bf16[128,256]{1,0:T(8,128)(2,1)} %refs_10_.5) | copy-start | bytes 196612
  4.0 5.2 %copy-start.1 = (bf16[128,256]{1,0:T(8,128)(2,1)S(1)}, bf16[128,256]{1,0:T(8,128)(2,1)}, u32[]{:S(2)}) copy-start(bf16[128,256]{1,0:T(8,128)(2,1)} %refs_11_.3) | copy-start | bytes 196612
  4.0 5.2 %copy-start.2 = (bf16[128,8,128]{2,1,0:T(8,128)(2,1)S(1)}, bf16[128,8,128]{2,1,0:T(8,128)(2,1)}, u32[]{:S(2)}) copy-start(bf16[128,8,128]{2,1,0:T(8,128)(2,1)} %param.10) | copy-start | bytes 786436
  4.0 5.2 %copy-start.3 = (bf16[128,128]{1,0:T(8,128)(2,1)S(1)}, bf16[128,128]{1,0:T(8,128)(2,1)}, u32[]{:S(2)}) copy-start(bf16[128,128]{1,0:T(8,128)(2,1)} %refs_9_.1) | copy-start | bytes 98308
  4.0 5.2 %copy-start.4 = (bf16[128,128]{1,0:T(8,128)(2,1)S(1)}, bf16[128,128]{1,0:T(8,128)(2,1)}, u32[]{:S(2)}) copy-start(bf16[128,128]{1,0:T(8,128)(2,1)} %refs_10_.3) | copy-start | bytes 98308
  5.1 9.0 %collective-permute-start.3 = (bf16[512,128]{1,0:T(8,128)(2,1)S(1)}, bf16[512,128]{1,0:T(8,128)(2,1)S(1)}, u32[]{:S(2)}, u32[]{:S(2)}) collective-permute-start(bf16[512,128]{1,0:T(8,128)(2,1)S(1)} %get-tuple-element.93), channel_id=1, source_target_pairs={{0,2},{1,3},{2,0},{3,1},{4,6},{5,7},{6,4},{7,5},{8,10},{9,11},{10,... | collective-permute-start | bytes 393224 | tf_op jit(solution)/shard_map/ppermute | solution.py:233
  5.6 8.9 %collective-permute-start.2 = (bf16[512,128]{1,0:T(8,128)(2,1)S(1)}, bf16[512,128]{1,0:T(8,128)(2,1)S(1)}, u32[]{:S(2)}, u32[]{:S(2)}) collective-permute-start(bf16[512,128]{1,0:T(8,128)(2,1)S(1)} %get-tuple-element.93), channel_id=1, source_target_pairs={{0,4},{1,5},{2,6},{3,7},{4,0},{5,1},{6,2},{7,3},{8,12},{9,13},{10,... | collective-permute-start | bytes 393224 | tf_op jit(solution)/shard_map/ppermute | solution.py:233
  5.7 11.3 %collective-permute-start.6 = (bf16[512,128]{1,0:T(8,128)(2,1)S(1)}, bf16[512,128]{1,0:T(8,128)(2,1)S(1)}, u32[]{:S(2)}, u32[]{:S(2)}) collective-permute-start(bf16[512,128]{1,0:T(8,128)(2,1)S(1)} %get-tuple-element.94), channel_id=1, source_target_pairs={{0,4},{1,5},{2,6},{3,7},{4,0},{5,1},{6,2},{7,3},{8,12},{9,13},{10,... | collective-permute-start | bytes 393224 | tf_op jit(solution)/shard_map/ppermute | solution.py:233
  7.7 9.3 %collective-permute-start.1 = (bf16[512,128]{1,0:T(8,128)(2,1)S(1)}, bf16[512,128]{1,0:T(8,128)(2,1)S(1)}, u32[]{:S(2)}, u32[]{:S(2)}) collective-permute-start(bf16[512,128]{1,0:T(8,128)(2,1)S(1)} %get-tuple-element.94), channel_id=1, source_target_pairs={{0,2},{1,3},{2,0},{3,1},{4,6},{5,7},{6,4},{7,5},{8,10},{9,11},{10,... | collective-permute-start | bytes 393224 | tf_op jit(solution)/shard_map/ppermute | solution.py:233
  9.2 0.7 %copy-start.8 = (f32[128]{0:T(128)S(1)}, f32[128]{0:T(128)}, u32[]{:S(2)}) copy-start(f32[128]{0:T(128)} %param.16) | copy-start | bytes 1540
  9.2 0.7 %copy-start.9 = (f32[128]{0:T(128)S(1)}, f32[128]{0:T(128)}, u32[]{:S(2)}) copy-start(f32[128]{0:T(128)} %param.17) | copy-start | bytes 1540
  9.2 0.7 %copy-start.5 = (f32[128]{0:T(128)S(1)}, f32[128]{0:T(128)}, u32[]{:S(2)}) copy-start(f32[128]{0:T(128)} %param.12) | copy-start | bytes 1540
  9.2 0.7 %copy-start.6 = (f32[128]{0:T(128)S(1)}, f32[128]{0:T(128)}, u32[]{:S(2)}) copy-start(f32[128]{0:T(128)} %param.13) | copy-start | bytes 1540
  9.2 0.7 %copy-start.7 = (s32[128]{0:T(128)S(1)}, s32[128]{0:T(128)}, u32[]{:S(2)}) copy-start(s32[128]{0:T(128)} %refs_1_.1) | copy-start | bytes 1540
  12.1 5.4 %collective-permute-start.8 = (bf16[1024,128]{1,0:T(8,128)(2,1)S(1)}, bf16[1024,128]{1,0:T(8,128)(2,1)S(1)}, u32[]{:S(2)}, u32[]{:S(2)}) collective-permute-start(bf16[1024,128]{1,0:T(8,128)(2,1)S(1)} %collective-permute-done.4.refs_3_.refs_5_), channel_id=1, source_target_pairs={{0,1},{1,0},{2,3},{3,2},{4,5},{5,4},{6,7},{7,6},{8,9},{9,8},{10,11... | collective-permute-start | bytes 786440 | tf_op jit(solution)/shard_map/ppermute | solution.py:233
  14.6 2.9 %collective-permute-start.9 = (bf16[512,128]{1,0:T(8,128)(2,1)S(1)}, bf16[512,128]{1,0:T(8,128)(2,1)S(1)}, u32[]{:S(2)}, u32[]{:S(2)}) collective-permute-start(bf16[512,128]{1,0:T(8,128)(2,1)S(1)} %collective-permute-done.2.refs_1_), channel_id=1, source_target_pairs={{0,1},{1,0},{2,3},{3,2},{4,5},{5,4},{6,7},{7,6},{8,9},{9,8},{10,11... | collective-permute-start | bytes 393224 | tf_op jit(solution)/shard_map/ppermute | solution.py:233
  14.6 2.9 %collective-permute-start.10 = (bf16[512,128]{1,0:T(8,128)(2,1)S(1)}, bf16[512,128]{1,0:T(8,128)(2,1)S(1)}, u32[]{:S(2)}, u32[]{:S(2)}) collective-permute-start(bf16[512,128]{1,0:T(8,128)(2,1)S(1)} %collective-permute-done.3.refs_2_), channel_id=1, source_target_pairs={{0,1},{1,0},{2,3},{3,2},{4,5},{5,4},{6,7},{7,6},{8,9},{9,8},{10,11... | collective-permute-start | bytes 393224 | tf_op jit(solution)/shard_map/ppermute | solution.py:233
  17.0 4.6 %collective-permute-start.5 = (bf16[512,128]{1,0:T(8,128)(2,1)S(1)}, bf16[512,128]{1,0:T(8,128)(2,1)S(1)}, u32[]{:S(2)}, u32[]{:S(2)}) collective-permute-start(bf16[512,128]{1,0:T(8,128)(2,1)S(1)} %collective-permute-done.1.refs_1_), channel_id=1, source_target_pairs={{0,1},{1,0},{2,3},{3,2},{4,5},{5,4},{6,7},{7,6},{8,9},{9,8},{10,11... | collective-permute-start | bytes 393224 | tf_op jit(solution)/shard_map/ppermute | solution.py:233
  17.0 4.6 %collective-permute-start.7 = (bf16[512,128]{1,0:T(8,128)(2,1)S(1)}, bf16[512,128]{1,0:T(8,128)(2,1)S(1)}, u32[]{:S(2)}, u32[]{:S(2)}) collective-permute-start(bf16[512,128]{1,0:T(8,128)(2,1)S(1)} %collective-permute-done.6.refs_3_), channel_id=1, source_target_pairs={{0,1},{1,0},{2,3},{3,2},{4,5},{5,4},{6,7},{7,6},{8,9},{9,8},{10,11... | collective-permute-start | bytes 393224 | tf_op jit(solution)/shard_map/ppermute | solution.py:233
  19.0 12.9 %collective-permute-start.12 = (bf16[512,128]{1,0:T(8,128)(2,1)S(1)}, bf16[512,128]{1,0:T(8,128)(2,1)S(1)}, u32[]{:S(2)}, u32[]{:S(2)}) collective-permute-start(bf16[512,128]{1,0:T(8,128)(2,1)S(1)} %get-tuple-element.92), channel_id=1, source_target_pairs={{0,8},{1,9},{2,10},{3,11},{4,12},{5,13},{6,14},{7,15},{8,0},{9,1},... | collective-permute-start | bytes 393224 | tf_op jit(solution)/shard_map/ppermute | solution.py:233
  23.7 10.1 %collective-permute-start.11 = (bf16[512,128]{1,0:T(8,128)(2,1)S(1)}, bf16[512,128]{1,0:T(8,128)(2,1)S(1)}, u32[]{:S(2)}, u32[]{:S(2)}) collective-permute-start(bf16[512,128]{1,0:T(8,128)(2,1)S(1)} %get-tuple-element.88), channel_id=1, source_target_pairs={{0,8},{1,9},{2,10},{3,11},{4,12},{5,13},{6,14},{7,15},{8,0},{9,1},... | collective-permute-start | bytes 393224 | tf_op jit(solution)/shard_map/ppermute | solution.py:233
